TPU v7x, 32 devices: a whole 2x2x4 slice. The times are simulated.
32 devices in a mesh: batch: 8 (over y, x, core), mp: 4 (over z).
Axes of the slice: x: 2, y: 2, z: 4, core: 2. Of those that a mesh axis runs over, the one named last changes fastest.
Arguments:
- residual: bfloat16 [8, 64, 8192], P('batch', None, 'mp'), may hold values from -6 to 6
- query_states: bfloat16 [8, 64, 4096], P('batch', None, 'mp')
- key_states: bfloat16 [8, 64, 512], P('batch')
- value_states: bfloat16 [8, 64, 512], P('batch'), may hold values from -6 to 6
- prompt_perm: int32 [8], replicated, may hold values from 0 to 7, each once
- ablated_heads: int32 [8], replicated, may hold values from 0 to 31, as said below
- out_weight: bfloat16 [4096, 8192], P('batch', 'mp'), may hold values from -0.09375 to 0.09375
- rms_gain: float32 [8192], P('mp'), may hold values from 0.1 to 1.9
- gate_weight: bfloat16 [8192, 14336], P('mp', 'batch'), may hold values from -0.0625 to 0.0625
- up_weight: bfloat16 [8192, 14336], P('mp', 'batch'), may hold values from -0.0625 to 0.0625
- down_weight: bfloat16 [14336, 8192], P('batch', 'mp'), may hold values from -0.046875 to 0.046875
Outputs:
- attn_out: bfloat16 [8, 64, 8192], P('batch', None, 'mp')
- mlp_out: bfloat16 [8, 64, 8192], P('batch', None, 'mp')
Inputs may be any that keep to these rules, and one draw needn't show every extreme that they name: `prompt_perm`: each prompt index appears exactly once. `ablated_heads`: 8 different head indices in any order, one of them 32 - 1.
All inputs are finite; a program needn't handle non-finite values.
Results may differ from a plain program's by a relative error of at most 0.035.
Values may be sent and summed in bfloat16 or wider, within the bound.
A program may use at most 128 MiB of HBM per device.

v0:
```python
import math

import jax
import jax.numpy as jnp
from jax import lax
from jax.sharding import PartitionSpec as P

D = 8192
HEADS = 32
KV = 4
HD = 128
ABLATED = 8


def local_heads(query_states, key_states, value_states):
    prompts_here, length, columns = query_states.shape
    head_count = columns // HD
    first_head = lax.axis_index("mp") * head_count
    owners = (first_head + jnp.arange(head_count)) // (HEADS // KV)
    query_four = query_states.reshape(prompts_here, length, head_count, HD)
    key_four = jnp.take(key_states.reshape(prompts_here, length, KV, HD), owners, axis=2)
    value_four = jnp.take(value_states.reshape(prompts_here, length, KV, HD), owners, axis=2)
    scores = jnp.einsum(
        "pshd,pthd->phst", query_four, key_four, preferred_element_type=jnp.float32
    ) / math.sqrt(HD)
    positions = jnp.arange(length)
    causal = positions[:, None] >= positions[None, :]
    scores = jnp.where(causal, scores, -1e30)
    highest = jnp.max(scores, axis=-1, keepdims=True)
    weights = jnp.exp(scores - highest)
    probability = (weights / jnp.sum(weights, axis=-1, keepdims=True)).astype(jnp.bfloat16)
    mixed_heads = jnp.einsum(
        "phst,pthd->pshd", probability, value_four, preferred_element_type=jnp.float32
    )
    return mixed_heads.astype(jnp.bfloat16).reshape(prompts_here, length, head_count * HD)


def body(
    residual,
    query_states,
    key_states,
    value_states,
    prompt_perm,
    ablated_heads,
    out_weight,
    rms_gain,
    gate_weight,
    up_weight,
    down_weight,
):
    prompts_here, length, model_cols = residual.shape
    local_rows = prompts_here * length
    head_block = local_heads(query_states, key_states, value_states)
    all_heads = lax.all_gather(head_block, "mp", axis=2, tiled=True)
    batch_index = lax.axis_index("batch")
    sources = jnp.take(prompt_perm, batch_index * prompts_here + jnp.arange(prompts_here))
    stacked = all_heads.reshape(prompts_here, length, HEADS, HD)
    picked_cols = jnp.take(stacked, ablated_heads, axis=2).reshape(
        prompts_here, length * ABLATED * HD
    )
    block_rows = lax.all_gather(picked_cols, "batch", axis=0, tiled=True)
    selector = (sources[:, None] == jnp.arange(block_rows.shape[0])[None, :]).astype(jnp.bfloat16)
    picked = jnp.dot(selector, block_rows, preferred_element_type=jnp.float32)
    picked_four = picked.astype(jnp.bfloat16).reshape(prompts_here, length, ABLATED, HD)
    placing = (jnp.arange(HEADS)[:, None] == ablated_heads[None, :]).astype(jnp.bfloat16)
    placed = jnp.einsum(
        "psad,ga->psgd", picked_four, placing, preferred_element_type=jnp.float32
    ).astype(jnp.bfloat16)
    chosen = jnp.any(jnp.arange(HEADS)[:, None] == ablated_heads[None, :], axis=1)
    mixed_heads = jnp.where(chosen[None, None, :, None], placed, stacked).reshape(
        local_rows, HEADS * HD
    )
    attn_float = jnp.dot(
        mixed_heads,
        lax.all_gather(out_weight, "batch", axis=0, tiled=True),
        preferred_element_type=jnp.float32,
    )
    attn_out = attn_float.astype(jnp.bfloat16)
    hidden_state = residual.reshape(local_rows, model_cols).astype(jnp.float32) + attn_float
    squares = lax.psum(jnp.sum(hidden_state * hidden_state, axis=1), "mp")
    inverse = lax.rsqrt(squares / D + 1e-05)
    normed = (hidden_state * inverse[:, None] * rms_gain[None, :]).astype(jnp.bfloat16)
    block_rows = lax.all_gather(normed, "batch", axis=0, tiled=True)
    gate_part = jnp.dot(block_rows, gate_weight, preferred_element_type=jnp.float32)
    up_part = jnp.dot(block_rows, up_weight, preferred_element_type=jnp.float32)
    partial_value = jnp.concatenate([gate_part, up_part], axis=1)
    slice_width = gate_weight.shape[1]
    summed = lax.psum(partial_value.astype(jnp.bfloat16), "mp").astype(jnp.float32)
    hidden = (jax.nn.silu(summed[:, :slice_width]) * summed[:, slice_width:]).astype(jnp.bfloat16)
    block_rows = hidden
    mlp_float = lax.psum_scatter(
        jnp.dot(block_rows, down_weight, preferred_element_type=jnp.float32).astype(jnp.bfloat16),
        "batch",
        scatter_dimension=0,
        tiled=True,
    )
    return (
        attn_out.reshape(prompts_here, length, model_cols),
        mlp_float.reshape(prompts_here, length, model_cols),
    )


def solution(mesh):
    placed = (
        P("batch", None, "mp"),
        P("batch", None, "mp"),
        P("batch", None, None),
        P("batch", None, None),
        P(),
        P(),
        P("batch", "mp"),
        P("mp"),
        P("mp", "batch"),
        P("mp", "batch"),
        P("batch", "mp"),
    )
    return jax.shard_map(
        body,
        mesh=mesh,
        in_specs=placed,
        out_specs=(P("batch", None, "mp"), P("batch", None, "mp")),
        check_vma=False,
    )
```

profile of v0, /device:TPU:0, one launch (start us, length us, event | category | flops | bytes accessed | tf_op | source)
XLA Modules:
  0.0 413.6 jit_solution(484651136919230348)
XLA Ops:
  7.3 0.7 compare_select_fusion.1
  7.9 0.7 compare_and_fusion.1
  8.6 0.9 copy.37
  9.6 0.6 gather_fusion.2
  10.2 0.3 fusion.7
  10.5 0.9 bitcast_bitcast_fusion.1
  11.4 0.6 gather_fusion.1
  12.0 0.3 fusion.9
  12.3 17.4 %all_gather.12 = bf16[1,64,4096]{2,1,0:T(8,128)(2,1)S(1)} all-gather(bf16[1,64,1024]{2,1,0:T(8,128)(2,1)S(1)} %bitcast.109), channel_id=1, replica_groups=mesh['batch'=8,'mp'=4] {'mp'}, dimensions={2}, use_global_device_ids=true | all-gather | bytes 655360 | tf_op jit(solution)/shard_map/all_gather | solution.py:54
  29.6 0.1 copy.38
  29.7 0.2 copy.30
  30.0 0.6 gather_fusion
  30.6 0.1 copy.31
  30.7 0.8 reshape.200
  31.6 0.7 all-gather.5.cloned.1.call-update
  32.3 0.6 dynamic-slice.2
  33.6 27.7 %all-gather.9.cloned.1.call-done = bf16[8,1,65536]{2,1,0:T(2,128)(2,1)} async-done(((bf16[1,1,65536]{2,1,0:T(2,128)(2,1)}), bf16[8,1,65536]{2,1,0:T(2,128)(2,1)}) %all-gather.9.cloned.1.call-update) | async-done | bytes 1048592 | tf_op jit(solution)/shard_map/all_gather | solution.py:61
  61.3 2.9 fusion.11
  64.2 0.4 fusion.10
  64.6 88.5 %all-gather.5.cloned.1.call-done = bf16[4096,2048]{1,0:T(8,128)(2,1)} async-done(((bf16[512,2048]{1,0:T(8,128)(2,1)}), bf16[4096,2048]{1,0:T(8,128)(2,1)}) %all-gather.5.cloned.1.call-update) | async-done | bytes 16777232 | tf_op jit(solution)/shard_map/all_gather | solution.py:75
  153.1 8.9 %multiply_reduce_fusion = (f32[64]{0:T(128)S(1)}, f32[64,2048]{1,0:T(8,128)S(1)}) fusion(bf16[1,64,2048]{2,1,0:T(8,128)(2,1)S(1)} %copy-done.2, bf16[4096,2048]{1,0:T(8,128)(2,1)} %all-gather.5.cloned.1.call-done, bf16[8,8,32,128]{3,2,1,0:T(8,128)(2,1)S(1)} %bitcast.106), kind=kOutput, calls=%fused_computation.29 | convolution fusion | flops 1074266112 | bytes 18088192 | tf_op jit(solution)/shard_map/dot_general | solution.py:73
  162.0 11.7 %psum.14 = f32[64]{0:T(128)S(1)} all-reduce(f32[64]{0:T(128)S(1)} %get-tuple-element.16), channel_id=1, replica_groups=mesh['batch'=8,'mp'=4] {'mp'}, use_global_device_ids=true, to_apply=%region_4.6 | all-reduce | flops 64 | bytes 512 | tf_op jit(solution)/shard_map/psum | solution.py:80
  173.7 0.8 multiply_convert_fusion
  174.6 0.2 all-reduce.2.cloned.1.call-start
  174.8 25.1 %all-gather.7.cloned.1.call-done = bf16[512,2048]{1,0:T(8,128)(2,1)} async-done(((bf16[64,2048]{1,0:T(8,128)(2,1)}), bf16[512,2048]{1,0:T(8,128)(2,1)}) %all-gather.7.cloned.1.call-update) | async-done | bytes 2097168 | tf_op jit(solution)/shard_map/all_gather | solution.py:83
  199.9 7.8 %convolution_convert_fusion.1 = bf16[512,1792]{1,0:T(8,128)(2,1)S(1)} fusion(bf16[512,2048]{1,0:T(8,128)(2,1)} %all-gather.7.cloned.1.call-done, bf16[2048,1792]{1,0:T(8,128)(2,1)} %param.22), kind=kOutput, calls=%fused_computation.8 | convolution fusion | flops 3759013888 | bytes 11272192 | tf_op jit(solution)/shard_map/dot_general | solution.py:85
  207.7 7.0 %convolution_convert_fusion.2 = bf16[512,1792]{1,0:T(8,128)(2,1)S(1)} fusion(bf16[512,2048]{1,0:T(8,128)(2,1)S(1)} %copy-done.5, bf16[2048,1792]{1,0:T(8,128)(2,1)} %param.21), kind=kOutput, calls=%fused_computation.9 | convolution fusion | flops 3759013888 | bytes 11272192 | tf_op jit(solution)/shard_map/dot_general | solution.py:84
  214.7 2.1 pad_maximum_fusion
  216.9 138.2 %all-reduce.2.cloned.1.call-done = bf16[512,3584]{1,0:T(8,128)(2,1)} async-done(((bf16[512,3584]{1,0:T(8,128)(2,1)}), bf16[512,3584]{1,0:T(8,128)(2,1)}) %all-reduce.2.cloned.1.call-update) | async-done | bytes 3670032 | tf_op jit(solution)/shard_map/psum | solution.py:88
  355.1 3.0 convert_element_type.62
  358.1 8.5 %convolution_convert_fusion = bf16[512,2048]{1,0:T(8,128)(2,1)} fusion(bf16[1792,2048]{1,0:T(8,128)(2,1)} %param.23, f32[512,3584]{1,0:T(8,128)S(1)} %convert_element_type.62), kind=kOutput, calls=%fused_computation.7 | convolution fusion | flops 3764649984 | bytes 16777216 | tf_op jit(solution)/shard_map/dot_general | solution.py:92
  366.7 40.4 %reduce-scatter.2.cloned.1.call-done = bf16[64,2048]{1,0:T(8,128)(2,1)} async-done(((bf16[512,2048]{1,0:T(8,128)(2,1)}), bf16[64,2048]{1,0:T(8,128)(2,1)}) %reduce-scatter.2.cloned.1.call-update) | async-done | bytes 262160 | tf_op jit(solution)/shard_map/reduce_scatter | solution.py:91
  (33 shorter events, 0.6 us)
Async XLA Ops:
  7.2 1.5 copy-start
  7.2 54.1 %all-gather.9.cloned.1.call-start = ((), (), s32[]{:S(2)}) async-start(), calls=%async_computation.5 | async-start | bytes 2359296 | tf_op jit(solution)/shard_map/all_gather | solution.py:61
  11.9 20.4 %copy-start.6 = (s32[8]{0:T(128)S(1)}, s32[8]{0:T(128)}, u32[]{:S(2)}) copy-start(s32[8]{0:T(128)} %param.17) | copy-start | bytes 100
  12.0 21.6 %copy-start.4 = (s32[8]{0:T(128)S(1)}, s32[8]{0:T(128)}, u32[]{:S(2)}) copy-start(s32[8]{0:T(128)} %param.18) | copy-start | bytes 100
  29.7 123.4 %copy-start.2 = (bf16[1,64,2048]{2,1,0:T(8,128)(2,1)S(1)}, bf16[1,64,2048]{2,1,0:T(8,128)(2,1)}, u32[]{:S(2)}) copy-start(bf16[1,64,2048]{2,1,0:T(8,128)(2,1)} %param.13) | copy-start | bytes 786436
  31.5 121.6 %all-gather.5.cloned.1.call-start = ((), (), s32[]{:S(2)}) async-start(), calls=%async_computation.1 | async-start | bytes 18874368 | tf_op jit(solution)/shard_map/all_gather | solution.py:75
  32.3 167.6 %all-gather.7.cloned.1.call-start = ((), (), s32[]{:S(2)}) async-start(), calls=%async_computation.2 | async-start | bytes 2359296 | tf_op jit(solution)/shard_map/all_gather | solution.py:83
  153.1 20.6 %copy-start.3 = (f32[2048]{0:T(1024)S(1)}, f32[2048]{0:T(1024)}, u32[]{:S(2)}) copy-start(f32[2048]{0:T(1024)} %param.20) | copy-start | bytes 24580
  174.6 180.5 %all-reduce.2.cloned.1.call-start = ((), (), s32[]{:S(2)}) async-start(), calls=%async_computation.3 | async-start | bytes 7340032 | tf_op jit(solution)/shard_map/psum | solution.py:88
  199.9 7.8 %copy-start.5 = (bf16[512,2048]{1,0:T(8,128)(2,1)S(1)}, bf16[512,2048]{1,0:T(8,128)(2,1)}, u32[]{:S(2)}) copy-start(bf16[512,2048]{1,0:T(8,128)(2,1)} %all-gather.7.cloned.1.call-done) | copy-start | bytes 6291460
  216.9 190.2 %reduce-scatter.2.cloned.1.call-start = ((), (), s32[]{:S(2)}) async-start(), calls=%async_computation.4 | async-start | bytes 2359296 | tf_op jit(solution)/shard_map/reduce_scatter | solution.py:91
  358.1 49.0 %copy-start.1 = (bf16[1,64,512]{2,1,0:T(8,128)(2,1)S(1)}, bf16[1,64,512]{2,1,0:T(8,128)(2,1)}, u32[]{:S(2)}) copy-start(bf16[1,64,512]{2,1,0:T(8,128)(2,1)} %param.15) | copy-start | bytes 196612
Sparse Core Ops, SparseCore 0:
  31.6 29.6 all-gather.8
  63.2 89.8 all-gather.4
  174.7 25.1 all-gather.6
  217.0 138.0 all-reduce.1
  366.8 40.2 reduce-scatter.1
where the time goes:
time: 414 us
  waiting for transfers between devices  321 us (78%)
  matrix products  36.1 us (9%)
  blocking collectives  29.1 us (7%)
  between operations  14.6 us (4%)
  other arithmetic  7.56 us (2%)
  local copies, waits for them, and re-layouts  5.31 us (1%)
    psum x1, waiting for transfers between devices, body(): lax.psum(partial_value.astype(jnp.bfloat16), 'mp').astype(jnp.float32)  138 us
    all_gather x1, waiting for transfers between devices, body(): lax.all_gather(out_weight, 'batch', axis=0, tiled=True)  88.5 us
    reduce_scatter x1, waiting for transfers between devices, body(): lax.psum_scatter(jnp.dot(block_rows, down_weight, preferred_element_type=...  40.4 us
    all_gather x1, waiting for transfers between devices, body(): block_rows = lax.all_gather(picked_cols, 'batch', axis=0, tiled=True)  27.7 us
    all_gather x1, waiting for transfers between devices, body(): block_rows = lax.all_gather(normed, 'batch', axis=0, tiled=True)  25.1 us
    all_gather x1, blocking collectives, body(): all_heads = lax.all_gather(head_block, 'mp', axis=2, tiled=True)  17.4 us
    psum x1, blocking collectives, body(): squares = lax.psum(jnp.sum(hidden_state * hidden_state, axis=1), 'mp')  11.7 us
    dot_general x1, matrix products, body(): jnp.dot(mixed_heads, lax.all_gather(out_weight, 'batch', axis=0, tiled=Tr...  8.92 us
  transfers between devices with their start and end apart: 5, of which 5 were waited for; matrix products, arithmetic and copies ran while one was open for 1% of the time, Pallas kernels for 0%

commit v1 on v0

v1 whole, which is shorter than its diff:
```python
import functools
import math

import jax
import jax.numpy as jnp
from jax import lax
from jax.experimental import pallas as pl
from jax.experimental.pallas import tpu as pltpu
from jax.sharding import PartitionSpec as P

D = 8192
HEADS = 32
KV = 4
HD = 128
ABLATED = 8


def heads_kernel(q_ref, k_ref, v_ref, o_ref):
    length = q_ref.shape[1]
    rows = lax.broadcasted_iota(jnp.int32, (length, length), 0)
    cols = lax.broadcasted_iota(jnp.int32, (length, length), 1)
    causal = rows >= cols
    for head in range(q_ref.shape[2] // HD):
        at = slice(head * HD, (head + 1) * HD)
        kv = slice(head * k_ref.shape[2] * HD // q_ref.shape[2] // HD * HD, None)
        kv = slice(kv.start, kv.start + HD)
        scores = lax.dot_general(
            q_ref[0, :, at],
            k_ref[0, :, kv],
            (((1,), (1,)), ((), ())),
            preferred_element_type=jnp.float32,
        ) / math.sqrt(HD)
        scores = jnp.where(causal, scores, -1e30)
        highest = jnp.max(scores, axis=-1, keepdims=True)
        weights = jnp.exp(scores - highest)
        probability = (weights / jnp.sum(weights, axis=-1, keepdims=True)).astype(jnp.bfloat16)
        o_ref[0, :, at] = jnp.dot(
            probability, v_ref[0, :, kv], preferred_element_type=jnp.float32
        ).astype(jnp.bfloat16)


def local_heads(query_states, key_states, value_states):
    prompts_here, length, columns = query_states.shape
    head_count = columns // HD
    group = HEADS // KV
    kv_count = max(1, head_count // group)
    first = lax.axis_index("mp") * head_count // group
    keys = lax.dynamic_slice_in_dim(key_states, first * HD, kv_count * HD, axis=2)
    values = lax.dynamic_slice_in_dim(value_states, first * HD, kv_count * HD, axis=2)
    spec = lambda width: pl.BlockSpec((1, length, width), lambda i: (i, 0, 0))
    return pl.pallas_call(
        heads_kernel,
        grid=(prompts_here,),
        in_specs=[spec(columns), spec(kv_count * HD), spec(kv_count * HD)],
        out_specs=spec(columns),
        out_shape=jax.ShapeDtypeStruct((prompts_here, length, columns), jnp.bfloat16),
    )(query_states, keys, values)


def body(
    residual,
    query_states,
    key_states,
    value_states,
    prompt_perm,
    ablated_heads,
    out_weight,
    rms_gain,
    gate_weight,
    up_weight,
    down_weight,
):
    prompts_here, length, model_cols = residual.shape
    local_rows = prompts_here * length
    batches = lax.axis_size("batch")
    head_block = local_heads(query_states, key_states, value_states)
    all_heads = lax.all_gather(head_block, "mp", axis=2, tiled=True)
    owned_cols = out_weight.shape[0]
    by_owner = all_heads.reshape(local_rows, batches, owned_cols).transpose(1, 0, 2)
    mine = lax.all_to_all(by_owner, "batch", 0, 0, tiled=True)
    prompts = batches * prompts_here
    mine = mine.reshape(prompts, length, owned_cols)
    swapped = jnp.concatenate(
        [lax.dynamic_slice_in_dim(mine, prompt_perm[p], 1, axis=0) for p in range(prompts)], axis=0
    )
    head_of_col = (lax.axis_index("batch") * owned_cols + jnp.arange(owned_cols)) // HD
    chosen = jnp.any(head_of_col[:, None] == ablated_heads[None, :], axis=1)
    ablated = jnp.where(chosen[None, None, :], swapped, mine).reshape(prompts * length, owned_cols)
    attn_part = jnp.dot(ablated, out_weight, preferred_element_type=jnp.float32)
    attn_sum = lax.psum_scatter(
        attn_part.astype(jnp.bfloat16), "batch", scatter_dimension=0, tiled=True
    )
    attn_float = attn_sum.astype(jnp.float32)
    attn_out = attn_sum
    hidden_state = residual.reshape(local_rows, model_cols).astype(jnp.float32) + attn_float
    squares = lax.psum(jnp.sum(hidden_state * hidden_state, axis=1), "mp")
    inverse = lax.rsqrt(squares / D + 1e-05)
    normed = (hidden_state * inverse[:, None] * rms_gain[None, :]).astype(jnp.bfloat16)
    block_rows = lax.all_gather(normed, "batch", axis=0, tiled=True)
    gate_part = jnp.dot(block_rows, gate_weight, preferred_element_type=jnp.float32)
    up_part = jnp.dot(block_rows, up_weight, preferred_element_type=jnp.float32)
    gate = lax.psum_scatter(
        gate_part.astype(jnp.bfloat16), "mp", scatter_dimension=0, tiled=True
    ).astype(jnp.float32)
    up = lax.psum_scatter(
        up_part.astype(jnp.bfloat16), "mp", scatter_dimension=0, tiled=True
    ).astype(jnp.float32)
    hidden = (jax.nn.silu(gate) * up).astype(jnp.bfloat16)
    hidden = lax.all_gather(hidden, "mp", axis=0, tiled=True)
    mlp_float = lax.psum_scatter(
        jnp.dot(hidden, down_weight, preferred_element_type=jnp.float32).astype(jnp.bfloat16),
        "batch",
        scatter_dimension=0,
        tiled=True,
    )
    return (
        attn_out.reshape(prompts_here, length, model_cols),
        mlp_float.reshape(prompts_here, length, model_cols),
    )


def solution(mesh):
    placed = (
        P("batch", None, "mp"),
        P("batch", None, "mp"),
        P("batch", None, None),
        P("batch", None, None),
        P(),
        P(),
        P("batch", "mp"),
        P("mp"),
        P("mp", "batch"),
        P("mp", "batch"),
        P("batch", "mp"),
    )
    return jax.shard_map(
        body,
        mesh=mesh,
        in_specs=placed,
        out_specs=(P("batch", None, "mp"), P("batch", None, "mp")),
        check_vma=False,
    )
```

time: 414 us -> 326 us (0.79)
  waiting for transfers between devices: 321 us -> 221 us
  between operations: 14.6 us -> 29.1 us
  matrix products: 36.1 us -> 29.4 us
    psum x1 -> x0, waiting for transfers between devices: 138 us -> none  [body(): lax.psum(partial_value.astype(jnp.bfloat16), 'mp').astype(jnp.float32)]
    reduce_scatter x1 -> x4, waiting for transfers between devices: 40.4 us -> 155 us  [the longest x1 43.5 us: body(): lax.psum_scatter(attn_part.astype(jnp.bfloat16), 'batch', scatter_dimensi...]
    all_gather x2 -> x1, waiting for transfers between devices: 116 us -> 40.5 us  [body(): hidden = lax.all_gather(hidden, 'mp', axis=0, tiled=True)]
    dot_general x6 -> x2, matrix products: 21.2 us -> 11.6 us  [the longest x1 8.98 us: body(): jnp.dot(hidden, down_weight, preferred_element_type=jnp.float32)]
  transfers between devices with their start and end apart: 5 -> 7, of which waited for: 5 -> 6; matrix products, arithmetic and copies ran while one was open for 1% -> 3% of each run, Pallas kernels for 0% -> 0%
where the time goes in v1:
time: 326 us
  waiting for transfers between devices  221 us (68%)
  matrix products  29.4 us (9%)
  blocking collectives  29.3 us (9%)
  between operations  29.1 us (9%)
  other arithmetic  5.29 us (2%)
  starting transfers between devices  4.15 us (1%)
  Pallas kernels  4.12 us (1%)
  local copies, waits for them, and re-layouts  3.41 us (1%)
    reduce_scatter x1, waiting for transfers between devices, body(): lax.psum_scatter(attn_part.astype(jnp.bfloat16), 'batch', scatter_dimensi...  43.5 us
    reduce_scatter x1, waiting for transfers between devices, body(): lax.psum_scatter(up_part.astype(jnp.bfloat16), 'mp', scatter_dimension=0,...  40.9 us
    all_gather x1, waiting for transfers between devices, body(): hidden = lax.all_gather(hidden, 'mp', axis=0, tiled=True)  40.5 us
    reduce_scatter x1, waiting for transfers between devices, body(): lax.psum_scatter(jnp.dot(hidden, down_weight, preferred_element_type=jnp....  40.3 us
    reduce_scatter x1, waiting for transfers between devices, body(): lax.psum_scatter(gate_part.astype(jnp.bfloat16), 'mp', scatter_dimension=...  30.5 us
    all_gather x1, waiting for transfers between devices, body(): block_rows = lax.all_gather(normed, 'batch', axis=0, tiled=True)  25.2 us
    all_gather x1, blocking collectives, body(): all_heads = lax.all_gather(head_block, 'mp', axis=2, tiled=True)  17.6 us
    psum x1, blocking collectives, body(): squares = lax.psum(jnp.sum(hidden_state * hidden_state, axis=1), 'mp')  11.7 us
  transfers between devices with their start and end apart: 7, of which 6 were waited for; matrix products, arithmetic and copies ran while one was open for 3% of the time, Pallas kernels for 0%

profile of v1, /device:TPU:0, one launch (start us, length us, event | category | flops | bytes accessed | tf_op | source)
XLA Modules:
  0.0 325.7 jit_solution(1508889582480531822)
XLA Ops:
  7.2 1.5 constant_dynamic-slice_fusion
  8.7 4.1 %shard_map.122 = bf16[1,64,1024]{2,1,0:T(8,128)(2,1)} custom-call(bf16[1,64,1024]{2,1,0:T(8,128)(2,1)} %q_ref.1, bf16[1,64,128]{2,1,0:T(8,128)(2,1)} %get-tuple-element.11.k_ref, bf16[1,64,128]{2,1,0:T(8,128)(2,1)} %get-tuple-element.10.v_ref), custom_call_target="tpu_custom_call" | custom-call | tf_op jit(solution)/shard_map/pallas_call | solution.py:51
  12.8 17.6 %all_gather.9 = bf16[1,64,4096]{2,1,0:T(8,128)(2,1)S(1)} all-gather(bf16[1,64,1024]{2,1,0:T(8,128)(2,1)} %shard_map.122), channel_id=1, replica_groups=mesh['batch'=8,'mp'=4] {'mp'}, dimensions={2}, use_global_device_ids=true | all-gather | bytes 655360 | tf_op jit(solution)/shard_map/all_gather | solution.py:77
  30.4 0.2 copy.15
  30.6 0.9 copy.17
  31.5 3.7 %all-to-all-start = ((bf16[8,64,512]{2,1,0:T(8,128)(2,1)}), bf16[8,64,512]{2,1,0:T(8,128)(2,1)S(1)}, u32[]{:S(2)}, u32[]{:S(2)}) async-start(bf16[8,64,512]{2,1,0:T(8,128)(2,1)} %bitcast.28), calls=%async_computation | async-start | bytes 1048576 | tf_op jit(solution)/shard_map/all_to_all | solution.py:80
  35.2 0.0 reduce-scatter.5.cloned.1.call-start
  35.3 0.7 fusion.8
  50.8 0.1 compare_reduce_fusion
  51.1 0.1 broadcast_select_fusion
  51.1 2.6 convolution_convert_fusion.3
  53.8 0.0 reduce-scatter.5.cloned.1.call-update
  53.8 0.0 all-gather.3.cloned.1.call-start
  53.8 43.5 %reduce-scatter.5.cloned.1.call-done = bf16[64,2048]{1,0:T(8,128)(2,1)} async-done(((bf16[512,2048]{1,0:T(8,128)(2,1)}), bf16[64,2048]{1,0:T(8,128)(2,1)}) %reduce-scatter.5.cloned.1.call-update) | async-done | bytes 262160 | tf_op jit(solution)/shard_map/reduce_scatter | solution.py:90
  97.3 1.1 multiply_reduce_fusion
  98.5 11.7 %psum.7 = f32[64]{0:T(128)S(1)} all-reduce(f32[64]{0:T(128)S(1)} %multiply_reduce_fusion), channel_id=1, replica_groups=mesh['batch'=8,'mp'=4] {'mp'}, use_global_device_ids=true, to_apply=%region_3.4 | all-reduce | flops 64 | bytes 512 | tf_op jit(solution)/shard_map/psum | solution.py:96
  110.2 1.8 multiply_convert_fusion
  112.0 0.0 all-gather.3.cloned.1.call-update
  112.0 0.0 reduce-scatter.7.cloned.1.call-start
  112.0 25.2 %all-gather.3.cloned.1.call-done = bf16[512,2048]{1,0:T(8,128)(2,1)} async-done(((bf16[64,2048]{1,0:T(8,128)(2,1)}), bf16[512,2048]{1,0:T(8,128)(2,1)}) %all-gather.3.cloned.1.call-update) | async-done | bytes 2097168 | tf_op jit(solution)/shard_map/all_gather | solution.py:99
  137.3 8.9 %convolution_convert_fusion.2 = bf16[512,1792]{1,0:T(8,128)(2,1)} fusion(bf16[512,2048]{1,0:T(8,128)(2,1)} %all-gather.3.cloned.1.call-done, bf16[2048,1792]{1,0:T(8,128)(2,1)} %param.19), kind=kOutput, calls=%fused_computation.2 | convolution fusion | flops 3759013888 | bytes 11272192 | tf_op jit(solution)/shard_map/dot_general | solution.py:100
  146.2 0.0 reduce-scatter.7.cloned.1.call-update
  146.2 0.0 reduce-scatter.9.cloned.1.call-start
  146.2 8.9 %convolution_convert_fusion.1 = bf16[512,1792]{1,0:T(8,128)(2,1)} fusion(bf16[512,2048]{1,0:T(8,128)(2,1)} %all-gather.3.cloned.1.call-done, bf16[2048,1792]{1,0:T(8,128)(2,1)} %param.20), kind=kOutput, calls=%fused_computation.1 | convolution fusion | flops 3759013888 | bytes 11272192 | tf_op jit(solution)/shard_map/dot_general | solution.py:101
  155.2 0.0 all-gather.5.cloned.1.call-start
  155.2 30.5 %reduce-scatter.7.cloned.1.call-done = bf16[128,1792]{1,0:T(8,128)(2,1)} async-done(((bf16[512,1792]{1,0:T(8,128)(2,1)}), bf16[128,1792]{1,0:T(8,128)(2,1)}) %reduce-scatter.7.cloned.1.call-update) | async-done | bytes 458768 | tf_op jit(solution)/shard_map/reduce_scatter | solution.py:102
  185.8 40.9 %reduce-scatter.9.cloned.1.call-done = bf16[128,1792]{1,0:T(8,128)(2,1)} async-done(((bf16[512,1792]{1,0:T(8,128)(2,1)}), bf16[128,1792]{1,0:T(8,128)(2,1)}) %reduce-scatter.9.cloned.1.call-update) | async-done | bytes 458768 | tf_op jit(solution)/shard_map/reduce_scatter | solution.py:105
  226.6 2.2 fusion.4
  228.9 0.2 reduce-scatter.11.cloned.1.call-start
  229.1 40.5 %all-gather.5.cloned.1.call-done = bf16[512,1792]{1,0:T(8,128)(2,1)} async-done(((bf16[128,1792]{1,0:T(8,128)(2,1)}), bf16[512,1792]{1,0:T(8,128)(2,1)}) %all-gather.5.cloned.1.call-update) | async-done | bytes 1835024 | tf_op jit(solution)/shard_map/all_gather | solution.py:109
  269.6 9.0 %convolution_convert_fusion = bf16[512,2048]{1,0:T(8,128)(2,1)} fusion(bf16[512,1792]{1,0:T(8,128)(2,1)} %all-gather.5.cloned.1.call-done, bf16[1792,2048]{1,0:T(8,128)(2,1)} %param.21), kind=kOutput, calls=%fused_computation | convolution fusion | flops 3759144960 | bytes 11272192 | tf_op jit(solution)/shard_map/dot_general | solution.py:111
  278.6 40.3 %reduce-scatter.11.cloned.1.call-done = bf16[64,2048]{1,0:T(8,128)(2,1)} async-done(((bf16[512,2048]{1,0:T(8,128)(2,1)}), bf16[64,2048]{1,0:T(8,128)(2,1)}) %reduce-scatter.11.cloned.1.call-update) | async-done | bytes 262160 | tf_op jit(solution)/shard_map/reduce_scatter | solution.py:110
  (24 shorter events, 0.2 us)
Async XLA Ops:
  7.2 44.0 %copy-start = (bf16[512,2048]{1,0:T(8,128)(2,1)S(1)}, bf16[512,2048]{1,0:T(8,128)(2,1)}, u32[]{:S(2)}) copy-start(bf16[512,2048]{1,0:T(8,128)(2,1)} %param.17) | copy-start | bytes 6291460
  7.2 28.1 %copy-start.2 = (s32[8]{0:T(128)S(1)}, s32[8]{0:T(128)}, u32[]{:S(2)}) copy-start(s32[8]{0:T(128)} %param.15) | copy-start | bytes 100
  8.7 42.1 %copy-start.4 = (s32[8]{0:T(128)S(1)}, s32[8]{0:T(128)}, u32[]{:S(2)}) copy-start(s32[8]{0:T(128)} %param.16) | copy-start | bytes 100
  31.5 19.4 %all-to-all-start = ((bf16[8,64,512]{2,1,0:T(8,128)(2,1)}), bf16[8,64,512]{2,1,0:T(8,128)(2,1)S(1)}, u32[]{:S(2)}, u32[]{:S(2)}) async-start(bf16[8,64,512]{2,1,0:T(8,128)(2,1)} %bitcast.28), calls=%async_computation | async-start | bytes 1048576 | tf_op jit(solution)/shard_map/all_to_all | solution.py:80
  35.2 62.1 %reduce-scatter.5.cloned.1.call-start = ((), (), s32[]{:S(2)}) async-start(), calls=%async_computation.5 | async-start | bytes 2359296 | tf_op jit(solution)/shard_map/reduce_scatter | solution.py:90
  53.8 43.6 %copy-start.1 = (bf16[1,64,2048]{2,1,0:T(8,128)(2,1)S(1)}, bf16[1,64,2048]{2,1,0:T(8,128)(2,1)}, u32[]{:S(2)}) copy-start(bf16[1,64,2048]{2,1,0:T(8,128)(2,1)} %param.11) | copy-start | bytes 786436
  53.8 56.4 %copy-start.3 = (f32[2048]{0:T(1024)S(1)}, f32[2048]{0:T(1024)}, u32[]{:S(2)}) copy-start(f32[2048]{0:T(1024)} %param.18) | copy-start | bytes 24580
  53.8 83.5 %all-gather.3.cloned.1.call-start = ((), (), s32[]{:S(2)}) async-start(), calls=%async_computation.6 | async-start | bytes 2359296 | tf_op jit(solution)/shard_map/all_gather | solution.py:99
  112.0 73.8 %reduce-scatter.7.cloned.1.call-start = ((), (), s32[]{:S(2)}) async-start(), calls=%async_computation.7 | async-start | bytes 2293760 | tf_op jit(solution)/shard_map/reduce_scatter | solution.py:102
  146.2 80.4 %reduce-scatter.9.cloned.1.call-start = ((), (), s32[]{:S(2)}) async-start(), calls=%async_computation.8 | async-start | bytes 2293760 | tf_op jit(solution)/shard_map/reduce_scatter | solution.py:105
  155.2 114.4 %all-gather.5.cloned.1.call-start = ((), (), s32[]{:S(2)}) async-start(), calls=%async_computation.9 | async-start | bytes 2293760 | tf_op jit(solution)/shard_map/all_gather | solution.py:109
  228.9 90.0 %reduce-scatter.11.cloned.1.call-start = ((), (), s32[]{:S(2)}) async-start(), calls=%async_computation.10 | async-start | bytes 2359296 | tf_op jit(solution)/shard_map/reduce_scatter | solution.py:110
Sparse Core Ops, SparseCore 0:
  53.9 43.3 reduce-scatter.4
  112.1 25.1 all-gather.2
  146.3 39.3 reduce-scatter.6
  188.0 38.5 reduce-scatter.8
  229.0 40.5 all-gather.4
  278.7 40.0 reduce-scatter.10

commit v2 on v1

--- a/solution.py
+++ b/solution.py
@@ -1,3 +1,4 @@
+import functools
 import functools
 import math
 
@@ -55,6 +56,175 @@
         out_specs=spec(columns),
         out_shape=jax.ShapeDtypeStruct((prompts_here, length, columns), jnp.bfloat16),
     )(query_states, keys, values)
+
+
+def params(collective_id=None):
+    return pltpu.CompilerParams(
+        collective_id=collective_id,
+        has_side_effects=collective_id is not None,
+        vmem_limit_bytes=40 * 2**20,
+    )
+
+
+def swap_kernel(perm_ref, chosen_ref, rows_ref, o_ref):
+    chosen = chosen_ref[...] > 0
+    for prompt in range(rows_ref.shape[0]):
+        own = rows_ref[prompt].astype(jnp.float32)
+        other = rows_ref[perm_ref[prompt]].astype(jnp.float32)
+        o_ref[prompt] = jnp.where(chosen, other, own).astype(jnp.bfloat16)
+
+
+def swap(prompt_perm, chosen, rows):
+    vmem = pl.BlockSpec(memory_space=pltpu.VMEM)
+    return pl.pallas_call(
+        swap_kernel,
+        in_specs=[pl.BlockSpec(memory_space=pltpu.SMEM), vmem, vmem],
+        out_specs=vmem,
+        out_shape=jax.ShapeDtypeStruct(rows.shape, rows.dtype),
+        compiler_params=params(),
+    )(prompt_perm, chosen, rows)
+
+
+def place(devices):
+    me = lax.axis_index("batch")
+    core = lax.rem(me, 2)
+    return devices // 2, lax.div(me, 2), core, me + 1 - 2 * core
+
+
+def greet(chips, chip, core, mate):
+    barrier = pltpu.get_barrier_semaphore()
+    for peer in [mate] + [2 * lax.rem(chip + k, chips) + core for k in range(1, chips)]:
+        pl.semaphore_signal(
+            barrier, inc=1, device_id={"batch": peer}, device_id_type=pl.DeviceIdType.MESH
+        )
+    pl.semaphore_wait(barrier, chips)
+
+
+def send(src, dst, send_sem, recv_sem, peer):
+    return pltpu.make_async_remote_copy(
+        src_ref=src,
+        dst_ref=dst,
+        send_sem=send_sem,
+        recv_sem=recv_sem,
+        device_id={"batch": peer},
+        device_id_type=pl.DeviceIdType.MESH,
+    )
+
+
+def scatter_kernel(x_ref, o_ref, near, part, far, send_near, recv_near, send_far, recv_far):
+    chips, chip, core, mate = place(x_ref.shape[0])
+    greet(chips, chip, core, mate)
+    owner = [lax.rem(chip + k, chips) for k in range(chips)]
+    order = list(range(1, chips)) + [0]
+    to_mate = {}
+    for k in order:
+        to_mate[k] = send(
+            x_ref.at[2 * owner[k] + 1 - core], near.at[k], send_near.at[k], recv_near.at[k], mate
+        )
+        to_mate[k].start()
+    away = []
+    for k in range(1, chips):
+        to_mate[k].wait_recv()
+        target = 2 * owner[k] + core
+        part[k - 1] = (x_ref[target].astype(jnp.float32) + near[k].astype(jnp.float32)).astype(
+            jnp.bfloat16
+        )
+        copy = send(
+            part.at[k - 1], far.at[k - 1], send_far.at[k - 1], recv_far.at[k - 1], target
+        )
+        copy.start()
+        away.append(copy)
+    to_mate[0].wait_recv()
+    total = x_ref[2 * chip + core].astype(jnp.float32) + near[0].astype(jnp.float32)
+    for k in range(1, chips):
+        away[k - 1].wait_recv()
+        total = total + far[k - 1].astype(jnp.float32)
+    o_ref[...] = total.astype(jnp.bfloat16)
+    for k in order:
+        to_mate[k].wait_send()
+    for copy in away:
+        copy.wait_send()
+
+
+def scatter_sum(x):
+    devices, rows, columns = x.shape
+    chips = devices // 2
+    vmem = pl.BlockSpec(memory_space=pltpu.VMEM)
+    return pl.pallas_call(
+        scatter_kernel,
+        in_specs=[vmem],
+        out_specs=vmem,
+        out_shape=jax.ShapeDtypeStruct((rows, columns), jnp.bfloat16),
+        scratch_shapes=[
+            pltpu.VMEM((chips, rows, columns), jnp.bfloat16),
+            pltpu.VMEM((chips - 1, rows, columns), jnp.bfloat16),
+            pltpu.VMEM((chips - 1, rows, columns), jnp.bfloat16),
+            pltpu.SemaphoreType.DMA((chips,)),
+            pltpu.SemaphoreType.DMA((chips,)),
+            pltpu.SemaphoreType.DMA((chips - 1,)),
+            pltpu.SemaphoreType.DMA((chips - 1,)),
+        ],
+        compiler_params=params(1),
+    )(x)
+
+
+def gather_kernel(devices, x_ref, q_ref, ox_ref, oq_ref, send_far, recv_far, send_near, recv_near):
+    chips, chip, core, mate = place(devices)
+    me = 2 * chip + core
+    greet(chips, chip, core, mate)
+    pairs = ((x_ref, ox_ref), (q_ref, oq_ref))
+    sent = []
+    for k in range(1, chips):
+        target = 2 * lax.rem(chip + k, chips) + core
+        for i, (src, dst) in enumerate(pairs):
+            copy = send(src, dst.at[me], send_far.at[k - 1, i], recv_far.at[k - 1, i], target)
+            copy.start()
+            sent.append(copy)
+    for i, (src, dst) in enumerate(pairs):
+        copy = send(src, dst.at[me], send_near.at[0, i], recv_near.at[0, i], mate)
+        copy.start()
+        sent.append(copy)
+    ox_ref[me] = x_ref[...]
+    oq_ref[me] = q_ref[...]
+    for k in range(1, chips):
+        source = 2 * lax.rem(chip + chips - k, chips) + core
+        for i, (src, dst) in enumerate(pairs):
+            send(
+                src, dst.at[source], send_far.at[k - 1, i], recv_far.at[k - 1, i], mate
+            ).wait_recv()
+            copy = send(
+                dst.at[source], dst.at[source], send_near.at[k, i], recv_near.at[k, i], mate
+            )
+            copy.start()
+            sent.append(copy)
+    for k in range(chips):
+        source = 2 * lax.rem(chip + chips - k, chips) + 1 - core
+        for i, (src, dst) in enumerate(pairs):
+            send(src, dst.at[source], send_near.at[k, i], recv_near.at[k, i], mate).wait_recv()
+    for copy in sent:
+        copy.wait_send()
+
+
+def gather_rows(x, squares):
+    devices = lax.axis_size("batch")
+    chips = devices // 2
+    vmem = pl.BlockSpec(memory_space=pltpu.VMEM)
+    return pl.pallas_call(
+        functools.partial(gather_kernel, devices),
+        in_specs=[vmem, vmem],
+        out_specs=[vmem, vmem],
+        out_shape=[
+            jax.ShapeDtypeStruct((devices, *x.shape), x.dtype),
+            jax.ShapeDtypeStruct((devices, *squares.shape), squares.dtype),
+        ],
+        scratch_shapes=[
+            pltpu.SemaphoreType.DMA((chips - 1, 2)),
+            pltpu.SemaphoreType.DMA((chips - 1, 2)),
+            pltpu.SemaphoreType.DMA((chips, 2)),
+            pltpu.SemaphoreType.DMA((chips, 2)),
+        ],
+        compiler_params=params(2),
+    )(x, squares)
 
 
 def body(
@@ -80,23 +250,19 @@
     mine = lax.all_to_all(by_owner, "batch", 0, 0, tiled=True)
     prompts = batches * prompts_here
     mine = mine.reshape(prompts, length, owned_cols)
-    swapped = jnp.concatenate(
-        [lax.dynamic_slice_in_dim(mine, prompt_perm[p], 1, axis=0) for p in range(prompts)], axis=0
-    )
     head_of_col = (lax.axis_index("batch") * owned_cols + jnp.arange(owned_cols)) // HD
     chosen = jnp.any(head_of_col[:, None] == ablated_heads[None, :], axis=1)
-    ablated = jnp.where(chosen[None, None, :], swapped, mine).reshape(prompts * length, owned_cols)
+    chosen = jnp.where(chosen, 1.0, 0.0).astype(jnp.float32)[None, :]
+    ablated = swap(prompt_perm, chosen, mine).reshape(prompts * length, owned_cols)
     attn_part = jnp.dot(ablated, out_weight, preferred_element_type=jnp.float32)
-    attn_sum = lax.psum_scatter(
-        attn_part.astype(jnp.bfloat16), "batch", scatter_dimension=0, tiled=True
-    )
-    attn_float = attn_sum.astype(jnp.float32)
-    attn_out = attn_sum
-    hidden_state = residual.reshape(local_rows, model_cols).astype(jnp.float32) + attn_float
-    squares = lax.psum(jnp.sum(hidden_state * hidden_state, axis=1), "mp")
-    inverse = lax.rsqrt(squares / D + 1e-05)
-    normed = (hidden_state * inverse[:, None] * rms_gain[None, :]).astype(jnp.bfloat16)
-    block_rows = lax.all_gather(normed, "batch", axis=0, tiled=True)
+    attn_out = scatter_sum(attn_part.astype(jnp.bfloat16).reshape(batches, local_rows, model_cols))
+    hidden_state = residual.reshape(local_rows, model_cols).astype(jnp.float32) + attn_out.astype(
+        jnp.float32
+    )
+    squares = jnp.sum(hidden_state * hidden_state, axis=1, keepdims=True)
+    scaled = (hidden_state * rms_gain[None, :]).astype(jnp.bfloat16)
+    block_rows, square_rows = gather_rows(scaled, jnp.broadcast_to(squares, (local_rows, 128)))
+    block_rows = block_rows.reshape(batches * local_rows, model_cols)
     gate_part = jnp.dot(block_rows, gate_weight, preferred_element_type=jnp.float32)
     up_part = jnp.dot(block_rows, up_weight, preferred_element_type=jnp.float32)
     gate = lax.psum_scatter(
@@ -105,14 +271,14 @@
     up = lax.psum_scatter(
         up_part.astype(jnp.bfloat16), "mp", scatter_dimension=0, tiled=True
     ).astype(jnp.float32)
-    hidden = (jax.nn.silu(gate) * up).astype(jnp.bfloat16)
+    share = gate.shape[0]
+    squares = lax.psum(square_rows[:, :, 0].reshape(batches * local_rows), "mp")
+    squares = lax.dynamic_slice_in_dim(squares, lax.axis_index("mp") * share, share)
+    inverse = lax.rsqrt(squares / D + 1e-05)[:, None]
+    hidden = (jax.nn.silu(gate * inverse) * (up * inverse)).astype(jnp.bfloat16)
     hidden = lax.all_gather(hidden, "mp", axis=0, tiled=True)
-    mlp_float = lax.psum_scatter(
-        jnp.dot(hidden, down_weight, preferred_element_type=jnp.float32).astype(jnp.bfloat16),
-        "batch",
-        scatter_dimension=0,
-        tiled=True,
-    )
+    mlp_part = jnp.dot(hidden, down_weight, preferred_element_type=jnp.float32)
+    mlp_float = scatter_sum(mlp_part.astype(jnp.bfloat16).reshape(batches, local_rows, model_cols))
     return (
         attn_out.reshape(prompts_here, length, model_cols),
         mlp_float.reshape(prompts_here, length, model_cols),

time: 326 us -> 247 us (0.76)
  waiting for transfers between devices: 221 us -> 109 us
  Pallas kernels: 4.12 us -> 55.3 us
  between operations: 29.1 us -> 13.9 us
  matrix products: 29.4 us -> 25.9 us
    reduce_scatter x2 -> x0, waiting for transfers between devices: 83.8 us -> none  [the longest x1 43.5 us: body(): lax.psum_scatter(attn_part.astype(jnp.bfloat16), 'batch', scatter_dimensi...]
    pallas_call x0 -> x4, Pallas kernels: none -> 51.2 us  [the longest x2 33 us: scatter_sum(): pl.pallas_call(scatter_kernel, in_specs=[vmem], out_specs=vmem, out_shape...]
    all_gather x1 -> x0, waiting for transfers between devices: 25.2 us -> none  [body(): block_rows = lax.all_gather(normed, 'batch', axis=0, tiled=True)]
    reduce_scatter x1, waiting for transfers between devices: 30.5 us -> 17.7 us  [body(): lax.psum_scatter(gate_part.astype(jnp.bfloat16), 'mp', scatter_dimension=...]
    all_to_all x1, waiting for transfers between devices: 0.01 us -> 9.57 us  [body(): mine = lax.all_to_all(by_owner, 'batch', 0, 0, tiled=True)]
  transfers between devices with their start and end apart: 7 -> 4, of which waited for: 6 -> 4; matrix products, arithmetic and copies ran while one was open for 3% -> 4% of each run, Pallas kernels for 0% -> 0%
where the time goes in v2:
time: 247 us
  waiting for transfers between devices  109 us (44%)
  Pallas kernels  55.3 us (22%)
  blocking collectives  30.7 us (12%)
  matrix products  25.9 us (10%)
  between operations  13.9 us (6%)
  local copies, waits for them, and re-layouts  5.67 us (2%)
  starting transfers between devices  3.84 us (2%)
  other arithmetic  2.72 us (1%)
    reduce_scatter x1, waiting for transfers between devices, body(): lax.psum_scatter(up_part.astype(jnp.bfloat16), 'mp', scatter_dimension=0,...  40.9 us
    all_gather x1, waiting for transfers between devices, body(): hidden = lax.all_gather(hidden, 'mp', axis=0, tiled=True)  40.7 us
    pallas_call x2, Pallas kernels, scatter_sum(): pl.pallas_call(scatter_kernel, in_specs=[vmem], out_specs=vmem, out_shape...  33 us
    reduce_scatter x1, waiting for transfers between devices, body(): lax.psum_scatter(gate_part.astype(jnp.bfloat16), 'mp', scatter_dimension=...  17.7 us
    all_gather x1, blocking collectives, body(): all_heads = lax.all_gather(head_block, 'mp', axis=2, tiled=True)  17.6 us
    pallas_call x1, Pallas kernels, gather_rows(): pl.pallas_call(functools.partial(gather_kernel, devices), in_specs=[vmem,...  17.5 us
    psum x1, blocking collectives, body(): squares = lax.psum(square_rows[:, :, 0].reshape(batches * local_rows), 'mp')  13.2 us
    all_to_all x1, waiting for transfers between devices, body(): mine = lax.all_to_all(by_owner, 'batch', 0, 0, tiled=True)  9.57 us
  transfers between devices with their start and end apart: 4, of which 4 were waited for; matrix products, arithmetic and copies ran while one was open for 4% of the time, Pallas kernels for 0%

profile of v2, /device:TPU:0, one launch (start us, length us, event | category | flops | bytes accessed | tf_op | source)
XLA Modules:
  0.0 247.0 jit_solution(5280340324772852961)
XLA Ops:
  7.2 1.5 constant_dynamic-slice_fusion
  8.7 4.1 %shard_map.122 = bf16[1,64,1024]{2,1,0:T(8,128)(2,1)} custom-call(bf16[1,64,1024]{2,1,0:T(8,128)(2,1)} %q_ref.1, bf16[1,64,128]{2,1,0:T(8,128)(2,1)} %get-tuple-element.9.k_ref, bf16[1,64,128]{2,1,0:T(8,128)(2,1)} %get-tuple-element.8.v_ref), custom_call_target="tpu_custom_call" | custom-call | tf_op jit(solution)/shard_map/pallas_call | solution.py:52
  12.8 17.6 %all_gather.6 = bf16[1,64,4096]{2,1,0:T(8,128)(2,1)S(1)} all-gather(bf16[1,64,1024]{2,1,0:T(8,128)(2,1)} %shard_map.122), channel_id=1, replica_groups=mesh['batch'=8,'mp'=4] {'mp'}, dimensions={2}, use_global_device_ids=true | all-gather | bytes 655360 | tf_op jit(solution)/shard_map/all_gather | solution.py:247
  30.4 0.2 copy.15
  30.6 0.9 copy.17
  31.5 3.7 %all-to-all-start = ((bf16[8,64,512]{2,1,0:T(8,128)(2,1)}), bf16[8,64,512]{2,1,0:T(8,128)(2,1)S(1)}, u32[]{:S(2)}, u32[]{:S(2)}) async-start(bf16[8,64,512]{2,1,0:T(8,128)(2,1)} %bitcast.24), calls=%async_computation | async-start | bytes 1048576 | tf_op jit(solution)/shard_map/all_to_all | solution.py:250
  35.2 0.0 reduce-scatter.3.cloned.1.call-start
  35.3 0.1 compare_reduce_fusion
  35.4 9.6 %all-to-all-done.rows_ref = bf16[8,64,512]{2,1,0:T(8,128)(2,1)S(1)} async-done(((bf16[8,64,512]{2,1,0:T(8,128)(2,1)}), bf16[8,64,512]{2,1,0:T(8,128)(2,1)S(1)}, u32[]{:S(2)}, u32[]{:S(2)}) %all-to-all-start) | async-done | bytes 524320 | tf_op jit(solution)/shard_map/all_to_all | solution.py:250
  45.0 0.7 shard_map.123
  45.7 1.3 convolution_convert_fusion.3
  46.9 16.1 %shard_map.124 = bf16[64,2048]{1,0:T(8,128)(2,1)S(1)} custom-call(bf16[8,64,2048]{2,1,0:T(8,128)(2,1)S(1)} %bitcast.26), custom_call_target="tpu_custom_call" | custom-call | tf_op jit(solution)/shard_map/pallas_call | solution.py:153
  63.0 0.2 multiply_reduce_fusion
  63.3 0.1 broadcast_in_dim.12.q_ref
  63.3 17.5 %shard_map.125 = (bf16[8,64,2048]{2,1,0:T(8,128)(2,1)S(1)}, f32[8,64,128]{2,1,0:T(8,128)S(1)}) custom-call(bf16[64,2048]{1,0:T(8,128)(2,1)S(1)} %get-tuple-element.7.x_ref, f32[64,128]{1,0:T(8,128)S(1)} %broadcast_in_dim.12.q_ref), custom_call_target="tpu_custom_call" | custom-call | tf_op jit(solution)/shard_map/pallas_call | solution.py:212
  80.9 1.3 copy-done.2
  82.2 8.1 %convolution_convert_fusion.2 = bf16[512,1792]{1,0:T(8,128)(2,1)} fusion(bf16[512,2048]{1,0:T(8,128)(2,1)S(1)} %bitcast.31, bf16[2048,1792]{1,0:T(8,128)(2,1)} %param.19), kind=kOutput, calls=%fused_computation.2 | convolution fusion | flops 3759013888 | bytes 11272192 | tf_op jit(solution)/shard_map/dot_general | solution.py:266
  90.4 0.0 reduce-scatter.5.cloned.1.call-start
  90.4 8.9 %convolution_convert_fusion.1 = bf16[512,1792]{1,0:T(8,128)(2,1)} fusion(bf16[512,2048]{1,0:T(8,128)(2,1)} %bitcast.32, bf16[2048,1792]{1,0:T(8,128)(2,1)} %param.20), kind=kOutput, calls=%fused_computation.1 | convolution fusion | flops 3759013888 | bytes 11272192 | tf_op jit(solution)/shard_map/dot_general | solution.py:267
  99.4 0.0 all-gather.2.cloned.1.call-start
  99.5 0.1 slice_reduce_fusion
  99.6 0.1 reshape_squeeze.3
  99.7 13.2 %psum.7 = f32[512]{0:T(512)S(1)} all-reduce(f32[512]{0:T(512)S(1)} %reshape_squeeze.3), channel_id=1, replica_groups=mesh['batch'=8,'mp'=4] {'mp'}, use_global_device_ids=true, to_apply=%region_3.4 | all-reduce | flops 512 | bytes 4096 | tf_op jit(solution)/shard_map/psum | solution.py:275
  112.8 0.1 add_rsqrt_fusion
  112.9 17.7 %reduce-scatter.3.cloned.1.call-done = bf16[128,1792]{1,0:T(8,128)(2,1)} async-done(((bf16[512,1792]{1,0:T(8,128)(2,1)}), bf16[128,1792]{1,0:T(8,128)(2,1)}) %reduce-scatter.3.cloned.1.call-update) | async-done | bytes 458768 | tf_op jit(solution)/shard_map/reduce_scatter | solution.py:268
  130.7 40.9 %reduce-scatter.5.cloned.1.call-done = bf16[128,1792]{1,0:T(8,128)(2,1)} async-done(((bf16[512,1792]{1,0:T(8,128)(2,1)}), bf16[128,1792]{1,0:T(8,128)(2,1)}) %reduce-scatter.5.cloned.1.call-update) | async-done | bytes 458768 | tf_op jit(solution)/shard_map/reduce_scatter | solution.py:271
  171.6 2.3 multiply_convert_fusion
  173.9 40.7 %all-gather.2.cloned.1.call-done = bf16[512,1792]{1,0:T(8,128)(2,1)} async-done(((bf16[128,1792]{1,0:T(8,128)(2,1)}), bf16[512,1792]{1,0:T(8,128)(2,1)}) %all-gather.2.cloned.1.call-update) | async-done | bytes 1835024 | tf_op jit(solution)/shard_map/all_gather | solution.py:279
  214.6 7.6 %convolution_convert_fusion = bf16[512,2048]{1,0:T(8,128)(2,1)S(1)} fusion(bf16[512,1792]{1,0:T(8,128)(2,1)} %all-gather.2.cloned.1.call-done, bf16[1792,2048]{1,0:T(8,128)(2,1)} %param.21), kind=kOutput, calls=%fused_computation | convolution fusion | flops 3759144960 | bytes 11272192 | tf_op jit(solution)/shard_map/dot_general | solution.py:280
  222.2 16.9 %shard_map.126 = bf16[64,2048]{1,0:T(8,128)(2,1)S(1)} custom-call(bf16[8,64,2048]{2,1,0:T(8,128)(2,1)S(1)} %bitcast.27), custom_call_target="tpu_custom_call" | custom-call | tf_op jit(solution)/shard_map/pallas_call | solution.py:153
  239.1 0.7 copy.20
  239.8 0.7 copy.21
  (16 shorter events, 0.1 us)
Async XLA Ops:
  7.2 38.5 %copy-start = (bf16[512,2048]{1,0:T(8,128)(2,1)S(1)}, bf16[512,2048]{1,0:T(8,128)(2,1)}, u32[]{:S(2)}) copy-start(bf16[512,2048]{1,0:T(8,128)(2,1)} %param.17) | copy-start | bytes 6291460
  7.2 28.1 %copy-start.5 = (s32[8]{0:T(128)S(1)}, s32[8]{0:T(128)}, u32[]{:S(2)}) copy-start(s32[8]{0:T(128)} %param.16) | copy-start | bytes 100
  7.2 37.8 %copy-start.1 = (s32[8]{0:T(128)S(1)}, s32[8]{0:T(128)}, u32[]{:S(2)}) copy-start(s32[8]{0:T(128)} %perm_ref.1) | copy-start | bytes 100
  31.5 13.5 %all-to-all-start = ((bf16[8,64,512]{2,1,0:T(8,128)(2,1)}), bf16[8,64,512]{2,1,0:T(8,128)(2,1)S(1)}, u32[]{:S(2)}, u32[]{:S(2)}) async-start(bf16[8,64,512]{2,1,0:T(8,128)(2,1)} %bitcast.24), calls=%async_computation | async-start | bytes 1048576 | tf_op jit(solution)/shard_map/all_to_all | solution.py:250
  35.2 95.4 %reduce-scatter.3.cloned.1.call-start = ((), (), s32[]{:S(2)}) async-start(), calls=%async_computation.3 | async-start | bytes 2293760 | tf_op jit(solution)/shard_map/reduce_scatter | solution.py:268
  46.9 16.1 %copy-start.3 = (bf16[1,64,2048]{2,1,0:T(8,128)(2,1)S(1)}, bf16[1,64,2048]{2,1,0:T(8,128)(2,1)}, u32[]{:S(2)}) copy-start(bf16[1,64,2048]{2,1,0:T(8,128)(2,1)} %param.11) | copy-start | bytes 786436
  46.9 16.1 %copy-start.4 = (f32[2048]{0:T(1024)S(1)}, f32[2048]{0:T(1024)}, u32[]{:S(2)}) copy-start(f32[2048]{0:T(1024)} %param.18) | copy-start | bytes 24580
  80.9 1.3 copy-start.2
  90.4 81.2 %reduce-scatter.5.cloned.1.call-start = ((), (), s32[]{:S(2)}) async-start(), calls=%async_computation.4 | async-start | bytes 2293760 | tf_op jit(solution)/shard_map/reduce_scatter | solution.py:271
  99.4 115.2 %all-gather.2.cloned.1.call-start = ((), (), s32[]{:S(2)}) async-start(), calls=%async_computation.5 | async-start | bytes 2293760 | tf_op jit(solution)/shard_map/all_gather | solution.py:279
Sparse Core Ops, SparseCore 0:
  90.5 40.1 reduce-scatter.2
  133.0 38.5 reduce-scatter.4
  174.0 40.5 all-gather.1

commit v3 on v2

--- a/solution.py
+++ b/solution.py
@@ -227,6 +227,203 @@
     )(x, squares)
 
 
+def hidden_kernel(
+    n, lag, x_ref, sq_ref, gate_ref, up_ref, o_ref, gate_buf, up_buf, own, got, squares,
+    weight_sem, send_sum, recv_sum, send_hid, recv_hid, send_sq, recv_sq,
+):
+    m = lax.axis_index("mp")
+    count, _, tokens, w = own.shape
+    half = tokens // 2
+    rows_of = (pl.ds(half, half), pl.ds(0, half))
+    last_of = (n - 1, 0)
+    pos_of = (m, n - 1 - m)
+    way_of = (1, -1)
+
+    def columns(c):
+        return pl.ds(0, w) if count == 1 else pl.ds(pl.multiple_of(c * w, w), w)
+
+    def fetch(c, slot):
+        return [
+            pltpu.make_async_copy(src.at[:, columns(c)], dst.at[slot], weight_sem.at[slot, i])
+            for i, (src, dst) in enumerate(((gate_ref, gate_buf), (up_ref, up_buf)))
+        ]
+
+    def remote(src, dst, send_sem, recv_sem, peer):
+        return pltpu.make_async_remote_copy(
+            src_ref=src,
+            dst_ref=dst,
+            send_sem=send_sem,
+            recv_sem=recv_sem,
+            device_id={"mp": peer},
+            device_id_type=pl.DeviceIdType.MESH,
+        )
+
+    def sum_copy(d, c, peer):
+        return remote(
+            own.at[c, :, rows_of[d], :],
+            got.at[d, c],
+            send_sum.at[d, c],
+            recv_sum.at[d, c],
+            peer,
+        )
+
+    def hid_copy(d, c, peer):
+        block = o_ref.at[rows_of[d], columns(c)]
+        return remote(block, block, send_hid.at[d, c], recv_hid.at[d, c], peer)
+
+    def sq_copy(d, slot):
+        return remote(
+            sq_ref.at[rows_of[d], :],
+            squares.at[slot],
+            send_sq.at[d],
+            recv_sq.at[slot],
+            last_of[d],
+        )
+
+    for copy in fetch(0, 0):
+        copy.start()
+    barrier = pltpu.get_barrier_semaphore()
+    for k in range(1, n):
+        pl.semaphore_signal(
+            barrier,
+            inc=1,
+            device_id={"mp": lax.rem(m + k, n)},
+            device_id_type=pl.DeviceIdType.MESH,
+        )
+    pl.semaphore_wait(barrier, n - 1)
+    for d in range(2):
+
+        @pl.when(m != last_of[d])
+        def _(d=d):
+            sq_copy(d, m).start()
+
+    def step(t, carry):
+        @pl.when(t < count)
+        def _():
+            slot = lax.rem(t, 2)
+            for copy in fetch(t, slot):
+                copy.wait()
+
+            @pl.when(t + 1 < count)
+            def _():
+                for copy in fetch(t + 1, 1 - slot):
+                    copy.start()
+
+            x = x_ref[...]
+            if w % 128 == 0:
+                both = jnp.concatenate([gate_buf[slot], up_buf[slot]], axis=1)
+                made = jnp.dot(x, both, preferred_element_type=jnp.float32).astype(jnp.bfloat16)
+                own[t, 0] = made[:, :w]
+                own[t, 1] = made[:, w:]
+            else:
+                for i, buf in enumerate((gate_buf, up_buf)):
+                    own[t, i] = jnp.dot(
+                        x, buf[slot], preferred_element_type=jnp.float32
+                    ).astype(jnp.bfloat16)
+
+        for d in range(2):
+            pos, rows, way = pos_of[d], rows_of[d], way_of[d]
+            c = t - lag * pos
+            here = (c >= 0) & (c < count)
+
+            @pl.when(here & (pos == 0))
+            def _(d=d, c=c, way=way):
+                sum_copy(d, c, m + way).start()
+
+            @pl.when(here & (pos > 0) & (pos < n - 1))
+            def _(d=d, c=c, way=way, rows=rows):
+                sum_copy(d, c, m - way).wait_recv()
+                own[c, :, rows, :] = (
+                    own[c, :, rows, :].astype(jnp.float32) + got[d, c].astype(jnp.float32)
+                ).astype(jnp.bfloat16)
+                sum_copy(d, c, m + way).start()
+
+            @pl.when(here & (pos == n - 1))
+            def _(d=d, c=c, way=way, rows=rows):
+                @pl.when(c == 0)
+                def _():
+                    for k in range(1, n):
+                        sq_copy(d, n - 1 - k if d == 0 else k).wait_recv()
+
+                total = sq_ref[rows, :]
+                for k in range(1, n):
+                    total = total + squares[n - 1 - k if d == 0 else k]
+                inverse = lax.rsqrt(total / D + 1e-05)[:, :1]
+                sum_copy(d, c, m - way).wait_recv()
+                summed = own[c, :, rows, :].astype(jnp.float32) + got[d, c].astype(jnp.float32)
+                gate = summed[0] * inverse
+                up = summed[1] * inverse
+                o_ref[rows, columns(c)] = (gate / (1.0 + jnp.exp(-gate)) * up).astype(jnp.bfloat16)
+                hid_copy(d, c, m - way).start()
+
+            back = t - lag * (2 * (n - 1) - pos)
+
+            @pl.when((back >= 0) & (back < count) & (pos < n - 1))
+            def _(d=d, back=back, way=way, pos=pos):
+                hid_copy(d, back, m + way).wait_recv()
+
+                @pl.when(pos > 0)
+                def _():
+                    hid_copy(d, back, m - way).start()
+
+        return carry
+
+    lax.fori_loop(0, count + 2 * lag * (n - 1), step, 0)
+
+    def finish(c, carry):
+        for d in range(2):
+            pos, way = pos_of[d], way_of[d]
+
+            @pl.when(pos < n - 1)
+            def _(d=d, way=way):
+                sum_copy(d, c, m + way).wait_send()
+
+            @pl.when(pos > 0)
+            def _(d=d, way=way):
+                hid_copy(d, c, m - way).wait_send()
+
+        return carry
+
+    lax.fori_loop(0, count, finish, 0)
+    for d in range(2):
+
+        @pl.when(m != last_of[d])
+        def _(d=d):
+            sq_copy(d, m).wait_send()
+
+
+def hidden_rows(x, squares, gate_weight, up_weight):
+    n = lax.axis_size("mp")
+    tokens, depth = x.shape
+    width = gate_weight.shape[1]
+    w = 128 if width % 128 == 0 else width
+    count = width // w
+    vmem = pl.BlockSpec(memory_space=pltpu.VMEM)
+    anywhere = pl.BlockSpec(memory_space=pl.ANY)
+    dma = pltpu.SemaphoreType.DMA
+    return pl.pallas_call(
+        functools.partial(hidden_kernel, n, 2 if count > 1 else 1),
+        in_specs=[vmem, vmem, anywhere, anywhere],
+        out_specs=vmem,
+        out_shape=jax.ShapeDtypeStruct((tokens, width), jnp.bfloat16),
+        scratch_shapes=[
+            pltpu.VMEM((2, depth, w), jnp.bfloat16),
+            pltpu.VMEM((2, depth, w), jnp.bfloat16),
+            pltpu.VMEM((count, 2, tokens, w), jnp.bfloat16),
+            pltpu.VMEM((2, count, 2, tokens // 2, w), jnp.bfloat16),
+            pltpu.VMEM((n, tokens // 2, 128), jnp.float32),
+            dma((2, 2)),
+            dma((2, count)),
+            dma((2, count)),
+            dma((2, count)),
+            dma((2, count)),
+            dma((2,)),
+            dma((n,)),
+        ],
+        compiler_params=params(3),
+    )(x, squares, gate_weight, up_weight)
+
+
 def body(
     residual,
     query_states,
@@ -263,20 +460,8 @@
     scaled = (hidden_state * rms_gain[None, :]).astype(jnp.bfloat16)
     block_rows, square_rows = gather_rows(scaled, jnp.broadcast_to(squares, (local_rows, 128)))
     block_rows = block_rows.reshape(batches * local_rows, model_cols)
-    gate_part = jnp.dot(block_rows, gate_weight, preferred_element_type=jnp.float32)
-    up_part = jnp.dot(block_rows, up_weight, preferred_element_type=jnp.float32)
-    gate = lax.psum_scatter(
-        gate_part.astype(jnp.bfloat16), "mp", scatter_dimension=0, tiled=True
-    ).astype(jnp.float32)
-    up = lax.psum_scatter(
-        up_part.astype(jnp.bfloat16), "mp", scatter_dimension=0, tiled=True
-    ).astype(jnp.float32)
-    share = gate.shape[0]
-    squares = lax.psum(square_rows[:, :, 0].reshape(batches * local_rows), "mp")
-    squares = lax.dynamic_slice_in_dim(squares, lax.axis_index("mp") * share, share)
-    inverse = lax.rsqrt(squares / D + 1e-05)[:, None]
-    hidden = (jax.nn.silu(gate * inverse) * (up * inverse)).astype(jnp.bfloat16)
-    hidden = lax.all_gather(hidden, "mp", axis=0, tiled=True)
+    square_rows = square_rows.reshape(batches * local_rows, 128)
+    hidden = hidden_rows(block_rows, square_rows, gate_weight, up_weight)
     mlp_part = jnp.dot(hidden, down_weight, preferred_element_type=jnp.float32)
     mlp_float = scatter_sum(mlp_part.astype(jnp.bfloat16).reshape(batches, local_rows, model_cols))
     return (

time: 247 us -> 179 us (0.72)
  waiting for transfers between devices: 109 us -> 9.63 us
  Pallas kernels: 55.3 us -> 136 us
  matrix products: 25.9 us -> 5.42 us
  blocking collectives: 30.7 us -> 17.6 us
  between operations: 13.9 us -> 0.86 us
    pallas_call x0 -> x1, Pallas kernels: none -> 82.6 us  [hidden_rows(): pl.pallas_call(functools.partial(hidden_kernel, n, 2 if count > 1 else 1)...]
    reduce_scatter x2 -> x0, waiting for transfers between devices: 58.6 us -> none  [the longest x1 40.9 us: body(): lax.psum_scatter(up_part.astype(jnp.bfloat16), 'mp', scatter_dimension=0,...]
    all_gather x1 -> x0, waiting for transfers between devices: 40.7 us -> none  [body(): hidden = lax.all_gather(hidden, 'mp', axis=0, tiled=True)]
    dot_general x2 -> x0, matrix products: 17.1 us -> none  [the longest x1 8.95 us: body(): up_part = jnp.dot(block_rows, up_weight, preferred_element_type=jnp.float32)]
    psum x1 -> x0, blocking collectives: 13.2 us -> none  [body(): squares = lax.psum(square_rows[:, :, 0].reshape(batches * local_rows), 'mp')]
    dot_general x1, matrix products: 7.6 us -> 4.16 us  [body(): mlp_part = jnp.dot(hidden, down_weight, preferred_element_type=jnp.float32)]
  transfers between devices with their start and end apart: 4 -> 1, of which waited for: 4 -> 1; matrix products, arithmetic and copies ran while one was open for 4% -> 0% of each run, Pallas kernels for 0% -> 0%
where the time goes in v3:
time: 179 us; the launch traced here: 178 us
  Pallas kernels  136 us (76%)
  blocking collectives  17.6 us (10%)
  waiting for transfers between devices  9.63 us (5%)
  matrix products  5.42 us (3%)
  local copies, waits for them, and re-layouts  4.16 us (2%)
  starting transfers between devices  3.72 us (2%)
    pallas_call x1, Pallas kernels, hidden_rows(): pl.pallas_call(functools.partial(hidden_kernel, n, 2 if count > 1 else 1)...  82.6 us
    pallas_call x2, Pallas kernels, scatter_sum(): pl.pallas_call(scatter_kernel, in_specs=[vmem], out_specs=vmem, out_shape...  31.5 us
    all_gather x1, blocking collectives, body(): all_heads = lax.all_gather(head_block, 'mp', axis=2, tiled=True)  17.6 us
    pallas_call x1, Pallas kernels, gather_rows(): pl.pallas_call(functools.partial(gather_kernel, devices), in_specs=[vmem,...  17.5 us
    all_to_all x1, waiting for transfers between devices, body(): mine = lax.all_to_all(by_owner, 'batch', 0, 0, tiled=True)  9.63 us
    dot_general x1, matrix products, body(): mlp_part = jnp.dot(hidden, down_weight, preferred_element_type=jnp.float32)  4.16 us
    pallas_call x1, Pallas kernels, local_heads(): pl.pallas_call(heads_kernel, grid=(prompts_here,), in_specs=[spec(columns...  4.11 us
    all_to_all x1, starting transfers between devices, body(): mine = lax.all_to_all(by_owner, 'batch', 0, 0, tiled=True)  3.72 us
  transfers between devices with their start and end apart: 1, of which 1 were waited for; matrix products, arithmetic and copies ran while one was open for 0% of the time, Pallas kernels for 0%

profile of v3, /device:TPU:0, one launch (start us, length us, event | category | flops | bytes accessed | tf_op | source)
XLA Modules:
  0.0 178.1 jit_solution(5531083743561998963)
XLA Ops:
  0.6 0.0 copy-start
  0.7 0.0 copy-start.4
  0.7 0.0 copy-start.1
  0.7 1.5 constant_dynamic-slice_fusion
  2.2 4.1 %shard_map.122 = bf16[1,64,1024]{2,1,0:T(8,128)(2,1)} custom-call(bf16[1,64,1024]{2,1,0:T(8,128)(2,1)} %q_ref.1, bf16[1,64,128]{2,1,0:T(8,128)(2,1)} %get-tuple-element.9.k_ref, bf16[1,64,128]{2,1,0:T(8,128)(2,1)} %get-tuple-element.8.v_ref), custom_call_target="tpu_custom_call" | custom-call | tf_op jit(solution)/shard_map/pallas_call | solution.py:52
  6.3 17.6 %all_gather.3 = bf16[1,64,4096]{2,1,0:T(8,128)(2,1)S(1)} all-gather(bf16[1,64,1024]{2,1,0:T(8,128)(2,1)} %shard_map.122), channel_id=1, replica_groups=mesh['batch'=8,'mp'=4] {'mp'}, dimensions={2}, use_global_device_ids=true | all-gather | bytes 655360 | tf_op jit(solution)/shard_map/all_gather | solution.py:444
  23.8 0.2 copy.15
  24.0 1.0 copy.17
  25.0 3.7 %all-to-all-start = ((bf16[8,64,512]{2,1,0:T(8,128)(2,1)}), bf16[8,64,512]{2,1,0:T(8,128)(2,1)S(1)}, u32[]{:S(2)}, u32[]{:S(2)}) async-start(bf16[8,64,512]{2,1,0:T(8,128)(2,1)} %bitcast.21), calls=%async_computation | async-start | bytes 1048576 | tf_op jit(solution)/shard_map/all_to_all | solution.py:447
  28.7 0.0 copy-done.4
  28.7 0.1 compare_reduce_fusion
  28.8 9.6 %all-to-all-done.rows_ref = bf16[8,64,512]{2,1,0:T(8,128)(2,1)S(1)} async-done(((bf16[8,64,512]{2,1,0:T(8,128)(2,1)}), bf16[8,64,512]{2,1,0:T(8,128)(2,1)S(1)}, u32[]{:S(2)}, u32[]{:S(2)}) %all-to-all-start) | async-done | bytes 524320 | tf_op jit(solution)/shard_map/all_to_all | solution.py:447
  38.4 0.0 copy-done.1
  38.5 0.7 shard_map.123
  39.1 0.0 copy-done
  39.1 0.0 slice-start.1
  39.1 1.3 convolution_convert_fusion.1
  40.4 0.0 copy-start.2
  40.4 0.0 copy-start.3
  40.4 16.1 %shard_map.124 = bf16[64,2048]{1,0:T(8,128)(2,1)S(1)} custom-call(bf16[8,64,2048]{2,1,0:T(8,128)(2,1)S(1)} %bitcast.26), custom_call_target="tpu_custom_call" | custom-call | tf_op jit(solution)/shard_map/pallas_call | solution.py:153
  56.5 0.0 copy-done.2
  56.5 0.0 copy-done.3
  56.5 0.0 slice-start.2
  56.5 0.2 multiply_reduce_fusion
  56.8 0.1 broadcast_in_dim.20.q_ref
  56.8 17.5 %shard_map.125 = (bf16[8,64,2048]{2,1,0:T(8,128)(2,1)S(1)}, f32[8,64,128]{2,1,0:T(8,128)S(1)}) custom-call(bf16[64,2048]{1,0:T(8,128)(2,1)S(1)} %get-tuple-element.7.x_ref, f32[64,128]{1,0:T(8,128)S(1)} %broadcast_in_dim.20.q_ref), custom_call_target="tpu_custom_call" | custom-call | tf_op jit(solution)/shard_map/pallas_call | solution.py:212
  74.4 0.0 slice-start.3
  74.4 82.6 %shard_map.126 = bf16[512,1792]{1,0:T(8,128)(2,1)S(1)} custom-call(bf16[512,2048]{1,0:T(8,128)(2,1)S(1)} %bitcast.25, f32[512,128]{1,0:T(8,128)S(1)} %bitcast.30, bf16[2048,1792]{1,0:T(8,128)(2,1)S(1)} %bitcast.23, bf16[2048,1792]{1,0:T(8,128)(2,1)} %up_ref.1), custom_call_target="tpu_custom_call" | custom-call | tf_op jit(solution)/shard_map/pallas_call | solution.py:404
  157.1 4.2 %convolution_convert_fusion = bf16[512,2048]{1,0:T(8,128)(2,1)S(1)} fusion(bf16[512,1792]{1,0:T(8,128)(2,1)S(1)} %shard_map.126, bf16[1792,2048]{1,0:T(8,128)(2,1)S(1)} %bitcast.35), kind=kOutput, calls=%fused_computation | convolution fusion | flops 3759144960 | bytes 11272192 | tf_op jit(solution)/shard_map/dot_general | solution.py:465
  161.3 15.4 %shard_map.127 = bf16[64,2048]{1,0:T(8,128)(2,1)S(1)} custom-call(bf16[8,64,2048]{2,1,0:T(8,128)(2,1)S(1)} %bitcast.27), custom_call_target="tpu_custom_call" | custom-call | tf_op jit(solution)/shard_map/pallas_call | solution.py:153
  176.7 0.7 copy.20
  177.4 0.7 copy.21
  (9 shorter events, 0.0 us)
Async XLA Ops:
  0.6 38.5 %copy-start = (bf16[512,2048]{1,0:T(8,128)(2,1)S(1)}, bf16[512,2048]{1,0:T(8,128)(2,1)}, u32[]{:S(2)}) copy-start(bf16[512,2048]{1,0:T(8,128)(2,1)} %param.17) | copy-start | bytes 6291460
  0.7 28.1 %copy-start.4 = (s32[8]{0:T(128)S(1)}, s32[8]{0:T(128)}, u32[]{:S(2)}) copy-start(s32[8]{0:T(128)} %param.16) | copy-start | bytes 100
  0.7 37.8 %copy-start.1 = (s32[8]{0:T(128)S(1)}, s32[8]{0:T(128)}, u32[]{:S(2)}) copy-start(s32[8]{0:T(128)} %perm_ref.1) | copy-start | bytes 100
  25.0 13.5 %all-to-all-start = ((bf16[8,64,512]{2,1,0:T(8,128)(2,1)}), bf16[8,64,512]{2,1,0:T(8,128)(2,1)S(1)}, u32[]{:S(2)}, u32[]{:S(2)}) async-start(bf16[8,64,512]{2,1,0:T(8,128)(2,1)} %bitcast.21), calls=%async_computation | async-start | bytes 1048576 | tf_op jit(solution)/shard_map/all_to_all | solution.py:447
  38.5 35.9 %slice-start = ((s8[7340032]{0:T(1024)(128)(4,1)}), s8[4194304]{0:T(1024)(128)(4,1)S(1)}, s32[]{:S(2)}) async-start(s8[7340032]{0:T(1024)(128)(4,1)} %bitcast.22), calls=%async_computation.1 | async-start | bytes 8388608
  39.1 35.3 %slice-start.1 = ((s8[7340032]{0:T(1024)(128)(4,1)}), s8[3145728]{0:T(1024)(128)(4,1)S(1)}, s32[]{:S(2)}) async-start(s8[7340032]{0:T(1024)(128)(4,1)} %bitcast.22), calls=%async_computation.2 | async-start | bytes 6291456
  40.4 16.1 %copy-start.2 = (bf16[1,64,2048]{2,1,0:T(8,128)(2,1)S(1)}, bf16[1,64,2048]{2,1,0:T(8,128)(2,1)}, u32[]{:S(2)}) copy-start(bf16[1,64,2048]{2,1,0:T(8,128)(2,1)} %param.11) | copy-start | bytes 786436
  40.4 16.1 %copy-start.3 = (f32[2048]{0:T(1024)S(1)}, f32[2048]{0:T(1024)}, u32[]{:S(2)}) copy-start(f32[2048]{0:T(1024)} %param.18) | copy-start | bytes 24580
  56.5 100.5 %slice-start.2 = ((s8[7340032]{0:T(1024)(128)(4,1)}), s8[4194304]{0:T(1024)(128)(4,1)S(1)}, s32[]{:S(2)}) async-start(s8[7340032]{0:T(1024)(128)(4,1)} %bitcast.34), calls=%async_computation.3 | async-start | bytes 8388608
  74.4 82.7 %slice-start.3 = ((s8[7340032]{0:T(1024)(128)(4,1)}), s8[3145728]{0:T(1024)(128)(4,1)S(1)}, s32[]{:S(2)}) async-start(s8[7340032]{0:T(1024)(128)(4,1)} %bitcast.34), calls=%async_computation.4 | async-start | bytes 6291456

commit v4 on v3

--- a/solution.py
+++ b/solution.py
@@ -16,46 +16,121 @@
 ABLATED = 8
 
 
-def heads_kernel(q_ref, k_ref, v_ref, o_ref):
-    length = q_ref.shape[1]
+def heads_kernel(q_ref, k_ref, v_ref, o_ref, blocks, send_line, recv_line, send_owner, recv_owner):
+    lines, owners, prompts, length, owned = blocks.shape
+    devices = o_ref.shape[0]
+    me, m = lax.axis_index("batch"), lax.axis_index("mp")
+    barrier = pltpu.get_barrier_semaphore()
+    for axis, at, size in (("mp", m, lines), ("batch", me, devices)):
+        for k in range(1, size):
+            pl.semaphore_signal(
+                barrier,
+                inc=1,
+                device_id={axis: lax.rem(at + k, size)},
+                device_id_type=pl.DeviceIdType.MESH,
+            )
     rows = lax.broadcasted_iota(jnp.int32, (length, length), 0)
     cols = lax.broadcasted_iota(jnp.int32, (length, length), 1)
     causal = rows >= cols
-    for head in range(q_ref.shape[2] // HD):
-        at = slice(head * HD, (head + 1) * HD)
-        kv = slice(head * k_ref.shape[2] * HD // q_ref.shape[2] // HD * HD, None)
-        kv = slice(kv.start, kv.start + HD)
-        scores = lax.dot_general(
-            q_ref[0, :, at],
-            k_ref[0, :, kv],
-            (((1,), (1,)), ((), ())),
-            preferred_element_type=jnp.float32,
-        ) / math.sqrt(HD)
-        scores = jnp.where(causal, scores, -1e30)
-        highest = jnp.max(scores, axis=-1, keepdims=True)
-        weights = jnp.exp(scores - highest)
-        probability = (weights / jnp.sum(weights, axis=-1, keepdims=True)).astype(jnp.bfloat16)
-        o_ref[0, :, at] = jnp.dot(
-            probability, v_ref[0, :, kv], preferred_element_type=jnp.float32
-        ).astype(jnp.bfloat16)
-
-
-def local_heads(query_states, key_states, value_states):
-    prompts_here, length, columns = query_states.shape
-    head_count = columns // HD
-    group = HEADS // KV
-    kv_count = max(1, head_count // group)
-    first = lax.axis_index("mp") * head_count // group
-    keys = lax.dynamic_slice_in_dim(key_states, first * HD, kv_count * HD, axis=2)
-    values = lax.dynamic_slice_in_dim(value_states, first * HD, kv_count * HD, axis=2)
-    spec = lambda width: pl.BlockSpec((1, length, width), lambda i: (i, 0, 0))
+    heads_here = q_ref.shape[2] // HD
+
+    def line_copy(source, k, j, peer):
+        block = blocks.at[source, j]
+        return pltpu.make_async_remote_copy(
+            src_ref=block,
+            dst_ref=block,
+            send_sem=send_line.at[k - 1, j],
+            recv_sem=recv_line.at[k - 1, j],
+            device_id={"mp": peer},
+            device_id_type=pl.DeviceIdType.MESH,
+        )
+
+    def owner_copy(source, k, j, slot, peer):
+        return pltpu.make_async_remote_copy(
+            src_ref=blocks.at[source, j],
+            dst_ref=o_ref.at[slot],
+            send_sem=send_owner.at[k, j],
+            recv_sem=recv_owner.at[slot],
+            device_id={"batch": peer},
+            device_id_type=pl.DeviceIdType.MESH,
+        )
+
+    def forward(source, k, j):
+        owner = source * owners + j
+
+        @pl.when(owner != me)
+        def _():
+            owner_copy(source, k, j, me, owner).start()
+
+        @pl.when(owner == me)
+        def _():
+            o_ref[me] = blocks[source, j]
+
+    for j in range(owners):
+        for at in range(0, owned, HD):
+            head = j * owned // HD + at // HD
+            kv = lax.div(m * heads_here + head, HEADS // KV)
+            kv = pl.ds(pl.multiple_of(kv * HD, HD), HD)
+            for prompt in range(prompts):
+                scores = lax.dot_general(
+                    q_ref[prompt, :, head * HD : (head + 1) * HD],
+                    k_ref[prompt, :, kv],
+                    (((1,), (1,)), ((), ())),
+                    preferred_element_type=jnp.float32,
+                ) / math.sqrt(HD)
+                scores = jnp.where(causal, scores, -1e30)
+                highest = jnp.max(scores, axis=-1, keepdims=True)
+                weights = jnp.exp(scores - highest)
+                probability = weights / jnp.sum(weights, axis=-1, keepdims=True)
+                blocks[m, j, prompt, :, at : at + HD] = jnp.dot(
+                    probability.astype(jnp.bfloat16),
+                    v_ref[prompt, :, kv],
+                    preferred_element_type=jnp.float32,
+                ).astype(jnp.bfloat16)
+        if j == 0:
+            pl.semaphore_wait(barrier, lines + devices - 2)
+        for k in range(1, lines):
+            line_copy(m, k, j, lax.rem(m + k, lines)).start()
+        forward(m, 0, j)
+    for k in range(1, lines):
+        source = lax.rem(m + lines - k, lines)
+        for j in range(owners):
+            line_copy(source, k, j, source).wait_recv()
+            forward(source, k, j)
+    for k in range(1, devices):
+        other = lax.rem(me + k, devices)
+        owner_copy(m, 0, 0, other, other).wait_recv()
+    for k in range(lines):
+        source = lax.rem(m + lines - k, lines)
+        for j in range(owners):
+            if k > 0:
+                line_copy(m, k, j, source).wait_send()
+
+            @pl.when(source * owners + j != me)
+            def _(source=source, k=k, j=j):
+                owner_copy(source, k, j, me, source * owners + j).wait_send()
+
+
+def owned_heads(query_states, key_states, value_states, owned):
+    prompts, length, columns = query_states.shape
+    devices, lines = lax.axis_size("batch"), lax.axis_size("mp")
+    owners = columns // owned
+    vmem = pl.BlockSpec(memory_space=pltpu.VMEM)
+    dma = pltpu.SemaphoreType.DMA
     return pl.pallas_call(
         heads_kernel,
-        grid=(prompts_here,),
-        in_specs=[spec(columns), spec(kv_count * HD), spec(kv_count * HD)],
-        out_specs=spec(columns),
-        out_shape=jax.ShapeDtypeStruct((prompts_here, length, columns), jnp.bfloat16),
-    )(query_states, keys, values)
+        in_specs=[vmem] * 3,
+        out_specs=vmem,
+        out_shape=jax.ShapeDtypeStruct((devices, prompts, length, owned), jnp.bfloat16),
+        scratch_shapes=[
+            pltpu.VMEM((lines, owners, prompts, length, owned), jnp.bfloat16),
+            dma((lines - 1, owners)),
+            dma((lines - 1, owners)),
+            dma((lines, owners)),
+            dma((devices,)),
+        ],
+        compiler_params=params(4),
+    )(query_states, key_states, value_states)
 
 
 def params(collective_id=None):
@@ -440,11 +515,8 @@
     prompts_here, length, model_cols = residual.shape
     local_rows = prompts_here * length
     batches = lax.axis_size("batch")
-    head_block = local_heads(query_states, key_states, value_states)
-    all_heads = lax.all_gather(head_block, "mp", axis=2, tiled=True)
     owned_cols = out_weight.shape[0]
-    by_owner = all_heads.reshape(local_rows, batches, owned_cols).transpose(1, 0, 2)
-    mine = lax.all_to_all(by_owner, "batch", 0, 0, tiled=True)
+    mine = owned_heads(query_states, key_states, value_states, owned_cols)
     prompts = batches * prompts_here
     mine = mine.reshape(prompts, length, owned_cols)
     head_of_col = (lax.axis_index("batch") * owned_cols + jnp.arange(owned_cols)) // HD

time: 179 us -> 166 us (0.927)
  Pallas kernels: 136 us -> 154 us
  blocking collectives: 17.6 us -> 0 us
  waiting for transfers between devices: 9.63 us -> 0 us
  starting transfers between devices: 3.72 us -> 0 us
    all_gather x1 -> x0, blocking collectives: 17.6 us -> none  [body(): all_heads = lax.all_gather(head_block, 'mp', axis=2, tiled=True)]
    pallas_call x1, Pallas kernels: 4.11 us -> 20.6 us  [owned_heads(): pl.pallas_call(heads_kernel, in_specs=[vmem] * 3, out_specs=vmem, out_sha...]
    all_to_all x1 -> x0, waiting for transfers between devices: 9.63 us -> none  [body(): mine = lax.all_to_all(by_owner, 'batch', 0, 0, tiled=True)]
    all_to_all x1 -> x0, starting transfers between devices: 3.72 us -> none  [body(): mine = lax.all_to_all(by_owner, 'batch', 0, 0, tiled=True)]
    unnamed x21 -> x24, local copies, waits for them, and re-layouts: 1.64 us -> 4.68 us
    pallas_call x2, Pallas kernels: 31.5 us -> 33.8 us  [scatter_sum(): pl.pallas_call(scatter_kernel, in_specs=[vmem], out_specs=vmem, out_shape...]
  transfers between devices with their start and end apart: 1 -> 0, of which waited for: 1 -> 0; matrix products, arithmetic and copies ran while one was open for 0% -> 0% of each run, Pallas kernels for 0% -> 0%
where the time goes in v4:
time: 166 us
  Pallas kernels  154 us (93%)
  matrix products  5.42 us (3%)
  local copies, waits for them, and re-layouts  4.75 us (3%)
    pallas_call x1, Pallas kernels, hidden_rows(): pl.pallas_call(functools.partial(hidden_kernel, n, 2 if count > 1 else 1)...  81.5 us
    pallas_call x2, Pallas kernels, scatter_sum(): pl.pallas_call(scatter_kernel, in_specs=[vmem], out_specs=vmem, out_shape...  33.8 us
    pallas_call x1, Pallas kernels, owned_heads(): pl.pallas_call(heads_kernel, in_specs=[vmem] * 3, out_specs=vmem, out_sha...  20.6 us
    pallas_call x1, Pallas kernels, gather_rows(): pl.pallas_call(functools.partial(gather_kernel, devices), in_specs=[vmem,...  17.4 us
    unnamed x24, local copies, waits for them, and re-layouts  4.68 us
    dot_general x1, matrix products, body(): mlp_part = jnp.dot(hidden, down_weight, preferred_element_type=jnp.float32)  4.16 us

profile of v4, /device:TPU:0, one launch (start us, length us, event | category | flops | bytes accessed | tf_op | source)
XLA Modules:
  0.0 165.9 jit_solution(4397786286263981394)
XLA Ops:
  0.6 0.0 copy-start
  0.7 0.9 compare_reduce_fusion
  1.6 0.0 copy-start.1
  1.6 0.9 copy-done.1
  2.5 0.0 copy-start.2
  2.5 0.8 copy-done.2
  3.3 0.8 copy-done.3
  4.1 20.6 %shard_map.122 = bf16[8,1,64,512]{3,2,1,0:T(8,128)(2,1)S(1)} custom-call(bf16[1,64,1024]{2,1,0:T(8,128)(2,1)S(1)} %copy-done.1, bf16[1,64,512]{2,1,0:T(8,128)(2,1)S(1)} %copy-done.2, bf16[1,64,512]{2,1,0:T(8,128)(2,1)S(1)} %copy-done.3), custom_call_target="tpu_custom_call" | custom-call | tf_op jit(solution)/shard_map/pallas_call | solution.py:120
  24.7 0.0 copy-start.4
  24.7 0.6 copy-done.4
  25.4 0.7 shard_map.123
  26.1 0.0 copy-done
  26.1 0.0 slice-start.1
  26.1 1.3 convolution_convert_fusion.1
  27.3 0.0 copy-start.5
  27.4 0.0 copy-start.6
  27.4 18.4 %shard_map.124 = bf16[64,2048]{1,0:T(8,128)(2,1)S(1)} custom-call(bf16[8,64,2048]{2,1,0:T(8,128)(2,1)S(1)} %bitcast.21), custom_call_target="tpu_custom_call" | custom-call | tf_op jit(solution)/shard_map/pallas_call | solution.py:228
  45.8 0.0 copy-done.5
  45.8 0.0 copy-done.6
  45.8 0.2 multiply_reduce_fusion
  46.0 0.1 broadcast_in_dim.20.q_ref
  46.1 17.4 %shard_map.125 = (bf16[8,64,2048]{2,1,0:T(8,128)(2,1)S(1)}, f32[8,64,128]{2,1,0:T(8,128)S(1)}) custom-call(bf16[64,2048]{1,0:T(8,128)(2,1)S(1)} %get-tuple-element.7.x_ref, f32[64,128]{1,0:T(8,128)S(1)} %broadcast_in_dim.20.q_ref), custom_call_target="tpu_custom_call" | custom-call | tf_op jit(solution)/shard_map/pallas_call | solution.py:287
  63.5 0.0 slice-done
  63.5 0.0 slice-done.1
  63.5 0.0 slice-start.3
  63.5 81.5 %shard_map.126 = bf16[512,1792]{1,0:T(8,128)(2,1)S(1)} custom-call(bf16[512,2048]{1,0:T(8,128)(2,1)S(1)} %bitcast.20, f32[512,128]{1,0:T(8,128)S(1)} %bitcast.26, bf16[2048,1792]{1,0:T(8,128)(2,1)S(1)} %bitcast.18, bf16[2048,1792]{1,0:T(8,128)(2,1)} %up_ref.1), custom_call_target="tpu_custom_call" | custom-call | tf_op jit(solution)/shard_map/pallas_call | solution.py:479
  145.0 0.0 slice-done.2
  145.0 0.0 slice-done.3
  145.0 4.2 %convolution_convert_fusion = bf16[512,2048]{1,0:T(8,128)(2,1)S(1)} fusion(bf16[512,1792]{1,0:T(8,128)(2,1)S(1)} %shard_map.126, bf16[1792,2048]{1,0:T(8,128)(2,1)S(1)} %bitcast.29), kind=kOutput, calls=%fused_computation | convolution fusion | flops 3759144960 | bytes 11272192 | tf_op jit(solution)/shard_map/dot_general | solution.py:537
  149.2 15.4 %shard_map.127 = bf16[64,2048]{1,0:T(8,128)(2,1)S(1)} custom-call(bf16[8,64,2048]{2,1,0:T(8,128)(2,1)S(1)} %bitcast.22), custom_call_target="tpu_custom_call" | custom-call | tf_op jit(solution)/shard_map/pallas_call | solution.py:228
  164.5 0.7 copy.15
  165.2 0.7 copy.16
  (7 shorter events, 0.0 us)
Async XLA Ops:
  0.6 25.4 %copy-start = (bf16[512,2048]{1,0:T(8,128)(2,1)S(1)}, bf16[512,2048]{1,0:T(8,128)(2,1)}, u32[]{:S(2)}) copy-start(bf16[512,2048]{1,0:T(8,128)(2,1)} %param.17) | copy-start | bytes 6291460
  1.6 0.9 copy-start.1
  2.5 0.8 copy-start.2
  3.3 0.8 copy-start.3
  24.7 0.7 copy-start.4
  25.4 38.1 %slice-start = ((s8[7340032]{0:T(1024)(128)(4,1)}), s8[4194304]{0:T(1024)(128)(4,1)S(1)}, s32[]{:S(2)}) async-start(s8[7340032]{0:T(1024)(128)(4,1)} %bitcast.17), calls=%async_computation | async-start | bytes 8388608
  26.1 37.4 %slice-start.1 = ((s8[7340032]{0:T(1024)(128)(4,1)}), s8[3145728]{0:T(1024)(128)(4,1)S(1)}, s32[]{:S(2)}) async-start(s8[7340032]{0:T(1024)(128)(4,1)} %bitcast.17), calls=%async_computation.1 | async-start | bytes 6291456
  27.3 18.4 %copy-start.5 = (bf16[1,64,2048]{2,1,0:T(8,128)(2,1)S(1)}, bf16[1,64,2048]{2,1,0:T(8,128)(2,1)}, u32[]{:S(2)}) copy-start(bf16[1,64,2048]{2,1,0:T(8,128)(2,1)} %param.11) | copy-start | bytes 786436
  27.4 18.4 %copy-start.6 = (f32[2048]{0:T(1024)S(1)}, f32[2048]{0:T(1024)}, u32[]{:S(2)}) copy-start(f32[2048]{0:T(1024)} %param.18) | copy-start | bytes 24580
  46.0 99.0 %slice-start.2 = ((s8[7340032]{0:T(1024)(128)(4,1)}), s8[4194304]{0:T(1024)(128)(4,1)S(1)}, s32[]{:S(2)}) async-start(s8[7340032]{0:T(1024)(128)(4,1)} %bitcast.28), calls=%async_computation.2 | async-start | bytes 8388608
  63.5 81.5 %slice-start.3 = ((s8[7340032]{0:T(1024)(128)(4,1)}), s8[3145728]{0:T(1024)(128)(4,1)S(1)}, s32[]{:S(2)}) async-start(s8[7340032]{0:T(1024)(128)(4,1)} %bitcast.28), calls=%async_computation.3 | async-start | bytes 6291456

commit v5 on v4

--- a/solution.py
+++ b/solution.py
@@ -190,40 +190,53 @@
     chips, chip, core, mate = place(x_ref.shape[0])
     greet(chips, chip, core, mate)
     owner = [lax.rem(chip + k, chips) for k in range(chips)]
-    order = list(range(1, chips)) + [0]
+    rows = x_ref.shape[1]
+    pieces = send_near.shape[1]
+    piece = rows // pieces
+    order = [(k, i) for k in (*range(1, chips), 0) for i in range(pieces)]
     to_mate = {}
-    for k in order:
-        to_mate[k] = send(
-            x_ref.at[2 * owner[k] + 1 - core], near.at[k], send_near.at[k], recv_near.at[k], mate
-        )
-        to_mate[k].start()
-    away = []
-    for k in range(1, chips):
-        to_mate[k].wait_recv()
+    for k, i in order:
+        at = pl.ds(i * piece, piece)
+        to_mate[k, i] = send(
+            x_ref.at[2 * owner[k] + 1 - core, at],
+            near.at[k, at],
+            send_near.at[k, i],
+            recv_near.at[k, i],
+            mate,
+        )
+        to_mate[k, i].start()
+    away = {}
+    for k, i in order:
+        at = pl.ds(i * piece, piece)
         target = 2 * owner[k] + core
-        part[k - 1] = (x_ref[target].astype(jnp.float32) + near[k].astype(jnp.float32)).astype(
-            jnp.bfloat16
-        )
-        copy = send(
-            part.at[k - 1], far.at[k - 1], send_far.at[k - 1], recv_far.at[k - 1], target
-        )
-        copy.start()
-        away.append(copy)
-    to_mate[0].wait_recv()
+        to_mate[k, i].wait_recv()
+        if k == 0:
+            continue
+        part[k - 1, at] = (
+            x_ref[target, at].astype(jnp.float32) + near[k, at].astype(jnp.float32)
+        ).astype(jnp.bfloat16)
+        away[k, i] = send(
+            part.at[k - 1, at],
+            far.at[k - 1, at],
+            send_far.at[k - 1, i],
+            recv_far.at[k - 1, i],
+            target,
+        )
+        away[k, i].start()
     total = x_ref[2 * chip + core].astype(jnp.float32) + near[0].astype(jnp.float32)
     for k in range(1, chips):
-        away[k - 1].wait_recv()
+        for i in range(pieces):
+            away[k, i].wait_recv()
         total = total + far[k - 1].astype(jnp.float32)
     o_ref[...] = total.astype(jnp.bfloat16)
-    for k in order:
-        to_mate[k].wait_send()
-    for copy in away:
+    for copy in (*to_mate.values(), *away.values()):
         copy.wait_send()
 
 
 def scatter_sum(x):
     devices, rows, columns = x.shape
     chips = devices // 2
+    pieces = 2 if rows % 32 == 0 else 1
     vmem = pl.BlockSpec(memory_space=pltpu.VMEM)
     return pl.pallas_call(
         scatter_kernel,
@@ -234,10 +247,10 @@
             pltpu.VMEM((chips, rows, columns), jnp.bfloat16),
             pltpu.VMEM((chips - 1, rows, columns), jnp.bfloat16),
             pltpu.VMEM((chips - 1, rows, columns), jnp.bfloat16),
-            pltpu.SemaphoreType.DMA((chips,)),
-            pltpu.SemaphoreType.DMA((chips,)),
-            pltpu.SemaphoreType.DMA((chips - 1,)),
-            pltpu.SemaphoreType.DMA((chips - 1,)),
+            pltpu.SemaphoreType.DMA((chips, pieces)),
+            pltpu.SemaphoreType.DMA((chips, pieces)),
+            pltpu.SemaphoreType.DMA((chips - 1, pieces)),
+            pltpu.SemaphoreType.DMA((chips - 1, pieces)),
         ],
         compiler_params=params(1),
     )(x)
@@ -303,7 +316,7 @@
 
 
 def hidden_kernel(
-    n, lag, x_ref, sq_ref, gate_ref, up_ref, o_ref, gate_buf, up_buf, own, got, squares,
+    n, lag, lag_back, x_ref, sq_ref, gate_ref, up_ref, o_ref, gate_buf, up_buf, own, got, squares,
     weight_sem, send_sum, recv_sum, send_hid, recv_hid, send_sq, recv_sq,
 ):
     m = lax.axis_index("mp")
@@ -431,7 +444,7 @@
                 o_ref[rows, columns(c)] = (gate / (1.0 + jnp.exp(-gate)) * up).astype(jnp.bfloat16)
                 hid_copy(d, c, m - way).start()
 
-            back = t - lag * (2 * (n - 1) - pos)
+            back = t - lag * (n - 1) - lag_back * (n - 1 - pos)
 
             @pl.when((back >= 0) & (back < count) & (pos < n - 1))
             def _(d=d, back=back, way=way, pos=pos):
@@ -443,7 +456,7 @@
 
         return carry
 
-    lax.fori_loop(0, count + 2 * lag * (n - 1), step, 0)
+    lax.fori_loop(0, count + (lag + lag_back) * (n - 1), step, 0)
 
     def finish(c, carry):
         for d in range(2):
@@ -477,7 +490,7 @@
     anywhere = pl.BlockSpec(memory_space=pl.ANY)
     dma = pltpu.SemaphoreType.DMA
     return pl.pallas_call(
-        functools.partial(hidden_kernel, n, 2 if count > 1 else 1),
+        functools.partial(hidden_kernel, n, 2 if count > 1 else 1, 1),
         in_specs=[vmem, vmem, anywhere, anywhere],
         out_specs=vmem,
         out_shape=jax.ShapeDtypeStruct((tokens, width), jnp.bfloat16),

time: 166 us -> 171 us (1.030)
  Pallas kernels: 154 us -> 158 us
    pallas_call x1, Pallas kernels: 81.5 us -> 85.8 us  [hidden_rows(): pl.pallas_call(functools.partial(hidden_kernel, n, 2 if count > 1 else 1,...]
where the time goes in v5:
time: 171 us; the launch traced here: 170 us
  Pallas kernels  158 us (92%)
  matrix products  5.42 us (3%)
  local copies, waits for them, and re-layouts  4.75 us (3%)
    pallas_call x1, Pallas kernels, hidden_rows(): pl.pallas_call(functools.partial(hidden_kernel, n, 2 if count > 1 else 1,...  85.8 us
    pallas_call x2, Pallas kernels, scatter_sum(): pl.pallas_call(scatter_kernel, in_specs=[vmem], out_specs=vmem, out_shape...  33.7 us
    pallas_call x1, Pallas kernels, owned_heads(): pl.pallas_call(heads_kernel, in_specs=[vmem] * 3, out_specs=vmem, out_sha...  20.6 us
    pallas_call x1, Pallas kernels, gather_rows(): pl.pallas_call(functools.partial(gather_kernel, devices), in_specs=[vmem,...  17.4 us
    unnamed x24, local copies, waits for them, and re-layouts  4.68 us
    dot_general x1, matrix products, body(): mlp_part = jnp.dot(hidden, down_weight, preferred_element_type=jnp.float32)  4.16 us

profile of v5, /device:TPU:0, one launch (start us, length us, event | category | flops | bytes accessed | tf_op | source)
XLA Modules:
  0.0 170.2 jit_solution(582821263185165880)
XLA Ops:
  0.6 0.0 copy-start
  0.7 0.9 compare_reduce_fusion
  1.6 0.0 copy-start.1
  1.6 0.9 copy-done.1
  2.5 0.8 copy-done.2
  3.3 0.8 copy-done.3
  4.1 20.6 %shard_map.122 = bf16[8,1,64,512]{3,2,1,0:T(8,128)(2,1)S(1)} custom-call(bf16[1,64,1024]{2,1,0:T(8,128)(2,1)S(1)} %copy-done.1, bf16[1,64,512]{2,1,0:T(8,128)(2,1)S(1)} %copy-done.2, bf16[1,64,512]{2,1,0:T(8,128)(2,1)S(1)} %copy-done.3), custom_call_target="tpu_custom_call" | custom-call | tf_op jit(solution)/shard_map/pallas_call | solution.py:120
  24.7 0.0 copy-start.4
  24.7 0.6 copy-done.4
  25.4 0.0 slice-start
  25.4 0.7 shard_map.123
  26.1 0.0 copy-done
  26.1 0.0 slice-start.1
  26.1 1.3 convolution_convert_fusion.1
  27.3 0.0 copy-start.5
  27.4 0.0 copy-start.6
  27.4 18.3 %shard_map.124 = bf16[64,2048]{1,0:T(8,128)(2,1)S(1)} custom-call(bf16[8,64,2048]{2,1,0:T(8,128)(2,1)S(1)} %bitcast.21), custom_call_target="tpu_custom_call" | custom-call | tf_op jit(solution)/shard_map/pallas_call | solution.py:241
  45.7 0.0 copy-done.5
  45.7 0.0 copy-done.6
  45.7 0.2 multiply_reduce_fusion
  45.9 0.1 broadcast_in_dim.20.q_ref
  46.0 17.4 %shard_map.125 = (bf16[8,64,2048]{2,1,0:T(8,128)(2,1)S(1)}, f32[8,64,128]{2,1,0:T(8,128)S(1)}) custom-call(bf16[64,2048]{1,0:T(8,128)(2,1)S(1)} %get-tuple-element.7.x_ref, f32[64,128]{1,0:T(8,128)S(1)} %broadcast_in_dim.20.q_ref), custom_call_target="tpu_custom_call" | custom-call | tf_op jit(solution)/shard_map/pallas_call | solution.py:300
  63.4 0.0 slice-done
  63.4 0.0 slice-done.1
  63.4 0.0 slice-start.3
  63.4 85.8 %shard_map.126 = bf16[512,1792]{1,0:T(8,128)(2,1)S(1)} custom-call(bf16[512,2048]{1,0:T(8,128)(2,1)S(1)} %bitcast.20, f32[512,128]{1,0:T(8,128)S(1)} %bitcast.26, bf16[2048,1792]{1,0:T(8,128)(2,1)S(1)} %bitcast.18, bf16[2048,1792]{1,0:T(8,128)(2,1)} %up_ref.1), custom_call_target="tpu_custom_call" | custom-call | tf_op jit(solution)/shard_map/pallas_call | solution.py:492
  149.3 0.0 slice-done.2
  149.3 0.0 slice-done.3
  149.3 4.2 %convolution_convert_fusion = bf16[512,2048]{1,0:T(8,128)(2,1)S(1)} fusion(bf16[512,1792]{1,0:T(8,128)(2,1)S(1)} %shard_map.126, bf16[1792,2048]{1,0:T(8,128)(2,1)S(1)} %bitcast.29), kind=kOutput, calls=%fused_computation | convolution fusion | flops 3759144960 | bytes 11272192 | tf_op jit(solution)/shard_map/dot_general | solution.py:550
  153.5 15.4 %shard_map.127 = bf16[64,2048]{1,0:T(8,128)(2,1)S(1)} custom-call(bf16[8,64,2048]{2,1,0:T(8,128)(2,1)S(1)} %bitcast.22), custom_call_target="tpu_custom_call" | custom-call | tf_op jit(solution)/shard_map/pallas_call | solution.py:241
  168.8 0.7 copy.15
  169.5 0.7 copy.16
  (7 shorter events, 0.0 us)
Async XLA Ops:
  0.6 25.4 %copy-start = (bf16[512,2048]{1,0:T(8,128)(2,1)S(1)}, bf16[512,2048]{1,0:T(8,128)(2,1)}, u32[]{:S(2)}) copy-start(bf16[512,2048]{1,0:T(8,128)(2,1)} %param.17) | copy-start | bytes 6291460
  1.6 0.9 copy-start.1
  2.5 0.8 copy-start.2
  3.3 0.8 copy-start.3
  24.7 0.7 copy-start.4
  25.4 38.0 %slice-start = ((s8[7340032]{0:T(1024)(128)(4,1)}), s8[4194304]{0:T(1024)(128)(4,1)S(1)}, s32[]{:S(2)}) async-start(s8[7340032]{0:T(1024)(128)(4,1)} %bitcast.17), calls=%async_computation | async-start | bytes 8388608
  26.1 37.3 %slice-start.1 = ((s8[7340032]{0:T(1024)(128)(4,1)}), s8[3145728]{0:T(1024)(128)(4,1)S(1)}, s32[]{:S(2)}) async-start(s8[7340032]{0:T(1024)(128)(4,1)} %bitcast.17), calls=%async_computation.1 | async-start | bytes 6291456
  27.3 18.4 %copy-start.5 = (bf16[1,64,2048]{2,1,0:T(8,128)(2,1)S(1)}, bf16[1,64,2048]{2,1,0:T(8,128)(2,1)}, u32[]{:S(2)}) copy-start(bf16[1,64,2048]{2,1,0:T(8,128)(2,1)} %param.11) | copy-start | bytes 786436
  27.4 18.4 %copy-start.6 = (f32[2048]{0:T(1024)S(1)}, f32[2048]{0:T(1024)}, u32[]{:S(2)}) copy-start(f32[2048]{0:T(1024)} %param.18) | copy-start | bytes 24580
  45.9 103.3 %slice-start.2 = ((s8[7340032]{0:T(1024)(128)(4,1)}), s8[4194304]{0:T(1024)(128)(4,1)S(1)}, s32[]{:S(2)}) async-start(s8[7340032]{0:T(1024)(128)(4,1)} %bitcast.28), calls=%async_computation.2 | async-start | bytes 8388608
  63.4 85.9 %slice-start.3 = ((s8[7340032]{0:T(1024)(128)(4,1)}), s8[3145728]{0:T(1024)(128)(4,1)S(1)}, s32[]{:S(2)}) async-start(s8[7340032]{0:T(1024)(128)(4,1)} %bitcast.28), calls=%async_computation.3 | async-start | bytes 6291456

commit v6 on v4

--- a/solution.py
+++ b/solution.py
@@ -477,7 +477,7 @@
     anywhere = pl.BlockSpec(memory_space=pl.ANY)
     dma = pltpu.SemaphoreType.DMA
     return pl.pallas_call(
-        functools.partial(hidden_kernel, n, 2 if count > 1 else 1),
+        functools.partial(hidden_kernel, n, 3 if count > 1 else 1),
         in_specs=[vmem, vmem, anywhere, anywhere],
         out_specs=vmem,
         out_shape=jax.ShapeDtypeStruct((tokens, width), jnp.bfloat16),

time: 166 us -> 170 us (1.024)
  Pallas kernels: 154 us -> 157 us
    pallas_call x1, Pallas kernels: 81.5 us -> 85 us  [hidden_rows(): pl.pallas_call(functools.partial(hidden_kernel, n, 3 if count > 1 else 1)...]
where the time goes in v6:
time: 170 us
  Pallas kernels  157 us (92%)
  matrix products  5.42 us (3%)
  local copies, waits for them, and re-layouts  4.75 us (3%)
    pallas_call x1, Pallas kernels, hidden_rows(): pl.pallas_call(functools.partial(hidden_kernel, n, 3 if count > 1 else 1)...  85 us
    pallas_call x2, Pallas kernels, scatter_sum(): pl.pallas_call(scatter_kernel, in_specs=[vmem], out_specs=vmem, out_shape...  33.8 us
    pallas_call x1, Pallas kernels, owned_heads(): pl.pallas_call(heads_kernel, in_specs=[vmem] * 3, out_specs=vmem, out_sha...  20.6 us
    pallas_call x1, Pallas kernels, gather_rows(): pl.pallas_call(functools.partial(gather_kernel, devices), in_specs=[vmem,...  17.4 us
    unnamed x24, local copies, waits for them, and re-layouts  4.68 us
    dot_general x1, matrix products, body(): mlp_part = jnp.dot(hidden, down_weight, preferred_element_type=jnp.float32)  4.17 us

profile of v6, /device:TPU:0, one launch (start us, length us, event | category | flops | bytes accessed | tf_op | source)
XLA Modules:
  0.0 169.5 jit_solution(2142735790543934962)
XLA Ops:
  0.6 0.0 copy-start
  0.7 0.9 compare_reduce_fusion
  1.6 0.0 copy-start.1
  1.6 0.9 copy-done.1
  2.5 0.0 copy-start.2
  2.5 0.8 copy-done.2
  3.3 0.8 copy-done.3
  4.1 20.6 %shard_map.122 = bf16[8,1,64,512]{3,2,1,0:T(8,128)(2,1)S(1)} custom-call(bf16[1,64,1024]{2,1,0:T(8,128)(2,1)S(1)} %copy-done.1, bf16[1,64,512]{2,1,0:T(8,128)(2,1)S(1)} %copy-done.2, bf16[1,64,512]{2,1,0:T(8,128)(2,1)S(1)} %copy-done.3), custom_call_target="tpu_custom_call" | custom-call | tf_op jit(solution)/shard_map/pallas_call | solution.py:120
  24.7 0.0 copy-start.4
  24.7 0.6 copy-done.4
  25.4 0.7 shard_map.123
  26.1 0.0 copy-done
  26.1 0.0 slice-start.1
  26.1 1.3 convolution_convert_fusion.1
  27.3 0.0 copy-start.5
  27.4 0.0 copy-start.6
  27.4 18.4 %shard_map.124 = bf16[64,2048]{1,0:T(8,128)(2,1)S(1)} custom-call(bf16[8,64,2048]{2,1,0:T(8,128)(2,1)S(1)} %bitcast.21), custom_call_target="tpu_custom_call" | custom-call | tf_op jit(solution)/shard_map/pallas_call | solution.py:228
  45.8 0.0 copy-done.5
  45.8 0.0 copy-done.6
  45.8 0.2 multiply_reduce_fusion
  46.0 0.1 broadcast_in_dim.20.q_ref
  46.1 17.4 %shard_map.125 = (bf16[8,64,2048]{2,1,0:T(8,128)(2,1)S(1)}, f32[8,64,128]{2,1,0:T(8,128)S(1)}) custom-call(bf16[64,2048]{1,0:T(8,128)(2,1)S(1)} %get-tuple-element.7.x_ref, f32[64,128]{1,0:T(8,128)S(1)} %broadcast_in_dim.20.q_ref), custom_call_target="tpu_custom_call" | custom-call | tf_op jit(solution)/shard_map/pallas_call | solution.py:287
  63.5 0.0 slice-done
  63.5 0.0 slice-done.1
  63.5 0.0 slice-start.3
  63.5 85.0 %shard_map.126 = bf16[512,1792]{1,0:T(8,128)(2,1)S(1)} custom-call(bf16[512,2048]{1,0:T(8,128)(2,1)S(1)} %bitcast.20, f32[512,128]{1,0:T(8,128)S(1)} %bitcast.26, bf16[2048,1792]{1,0:T(8,128)(2,1)S(1)} %bitcast.18, bf16[2048,1792]{1,0:T(8,128)(2,1)} %up_ref.1), custom_call_target="tpu_custom_call" | custom-call | tf_op jit(solution)/shard_map/pallas_call | solution.py:479
  148.5 0.0 slice-done.2
  148.5 0.0 slice-done.3
  148.6 4.2 %convolution_convert_fusion = bf16[512,2048]{1,0:T(8,128)(2,1)S(1)} fusion(bf16[512,1792]{1,0:T(8,128)(2,1)S(1)} %shard_map.126, bf16[1792,2048]{1,0:T(8,128)(2,1)S(1)} %bitcast.29), kind=kOutput, calls=%fused_computation | convolution fusion | flops 3759144960 | bytes 11272192 | tf_op jit(solution)/shard_map/dot_general | solution.py:537
  152.7 15.4 %shard_map.127 = bf16[64,2048]{1,0:T(8,128)(2,1)S(1)} custom-call(bf16[8,64,2048]{2,1,0:T(8,128)(2,1)S(1)} %bitcast.22), custom_call_target="tpu_custom_call" | custom-call | tf_op jit(solution)/shard_map/pallas_call | solution.py:228
  168.1 0.7 copy.15
  168.8 0.7 copy.16
  (7 shorter events, 0.0 us)
Async XLA Ops:
  0.6 25.4 %copy-start = (bf16[512,2048]{1,0:T(8,128)(2,1)S(1)}, bf16[512,2048]{1,0:T(8,128)(2,1)}, u32[]{:S(2)}) copy-start(bf16[512,2048]{1,0:T(8,128)(2,1)} %param.17) | copy-start | bytes 6291460
  1.6 0.9 copy-start.1
  2.5 0.8 copy-start.2
  3.3 0.8 copy-start.3
  24.7 0.7 copy-start.4
  25.4 38.1 %slice-start = ((s8[7340032]{0:T(1024)(128)(4,1)}), s8[4194304]{0:T(1024)(128)(4,1)S(1)}, s32[]{:S(2)}) async-start(s8[7340032]{0:T(1024)(128)(4,1)} %bitcast.17), calls=%async_computation | async-start | bytes 8388608
  26.1 37.4 %slice-start.1 = ((s8[7340032]{0:T(1024)(128)(4,1)}), s8[3145728]{0:T(1024)(128)(4,1)S(1)}, s32[]{:S(2)}) async-start(s8[7340032]{0:T(1024)(128)(4,1)} %bitcast.17), calls=%async_computation.1 | async-start | bytes 6291456
  27.3 18.4 %copy-start.5 = (bf16[1,64,2048]{2,1,0:T(8,128)(2,1)S(1)}, bf16[1,64,2048]{2,1,0:T(8,128)(2,1)}, u32[]{:S(2)}) copy-start(bf16[1,64,2048]{2,1,0:T(8,128)(2,1)} %param.11) | copy-start | bytes 786436
  27.4 18.4 %copy-start.6 = (f32[2048]{0:T(1024)S(1)}, f32[2048]{0:T(1024)}, u32[]{:S(2)}) copy-start(f32[2048]{0:T(1024)} %param.18) | copy-start | bytes 24580
  46.0 102.5 %slice-start.2 = ((s8[7340032]{0:T(1024)(128)(4,1)}), s8[4194304]{0:T(1024)(128)(4,1)S(1)}, s32[]{:S(2)}) async-start(s8[7340032]{0:T(1024)(128)(4,1)} %bitcast.28), calls=%async_computation.2 | async-start | bytes 8388608
  63.5 85.1 %slice-start.3 = ((s8[7340032]{0:T(1024)(128)(4,1)}), s8[3145728]{0:T(1024)(128)(4,1)S(1)}, s32[]{:S(2)}) async-start(s8[7340032]{0:T(1024)(128)(4,1)} %bitcast.28), calls=%async_computation.3 | async-start | bytes 6291456
